TPU v7x, 128 devices: a whole 4x4x4 slice. The times are simulated.
128 devices in a mesh: tok: 16 (over y, z), voc: 8 (over x, core).
Axes of the slice: x: 4, y: 4, z: 4, core: 2. Of those that a mesh axis runs over, the one named last changes fastest.
Arguments:
- hidden: bfloat16 [2048, 3584], P('tok', 'voc'), may hold values from -36 to 36
- weight: bfloat16 [3584, 256000], P(None, ('voc', 'tok')), may hold values from -1 to 1
- targets: int32 [2048], replicated, may hold values from 0 to 255999
- slot: int32 [16], replicated, may hold values from 0 to 15, each once
- prompt_len: int32 [16], replicated, may hold values from 1 to 64
- ref_means: float32 [16], replicated, may hold values from -17 to -13
Outputs:
- token_logprobs: float32 [2048], P('tok')
- margins: float32 [8], replicated
- loss: float32 [], replicated
All inputs are finite; a program needn't handle non-finite values.
Results may differ from a plain program's by a relative error of at most 0.0003.
Values may be sent and summed in bfloat16 or wider, within the bound.
No kernel may reach another device: no remote copies, remote signals or barrier semaphores. Data moves between devices by JAX's collectives and lax.ppermute only.
A program may use at most 128 MiB of HBM per device.

v0:
```python
import jax
import jax.numpy as jnp
from jax import lax
from jax.sharding import Mesh
from jax.sharding import PartitionSpec as P

VOC = ("voc_0", "voc_1")
TOK = ("tok_0", "tok_1")
VOC_TOK = ("voc_0", "voc_1", "tok_0", "tok_1")


beta_scale = 2.0


def sent_to_all(shard, axis):
    copies = jnp.broadcast_to(shard, (lax.axis_size(axis), *shard.shape))
    return lax.all_to_all(copies, axis, split_axis=0, concat_axis=0, tiled=True)


def joined_along(parts, dim):
    shape = list(parts.shape[1:])
    shape[dim] *= parts.shape[0]
    return jnp.moveaxis(parts, 0, dim).reshape(shape)


def collect(shard, axis, dim):
    parts = sent_to_all(shard, axis)
    return joined_along(parts, dim)


def gathered_once(shard, axis):
    leaves = jax.tree.leaves(shard)
    sequence = sorted(range(len(leaves)), key=lambda k: -leaves[k].size)
    width = (1, *leaves[sequence[0]].shape)[-1]
    lines = [
        jnp.pad(leaves[k].reshape(-1), (0, -leaves[k].size % width)).reshape(-1, width)
        for k in sequence
    ]
    both, at, found = (lax.all_gather(jnp.concatenate(lines), axis), 0, {})
    for k, line in zip(sequence, lines):
        section = both[:, at : at + len(line)].reshape(len(both), -1)
        found[k] = section[:, : leaves[k].size].reshape(-1, *leaves[k].shape)
        at += len(line)
    numbers = iter(range(len(leaves)))
    return jax.tree.map(lambda _: found[next(numbers)], shard)


def merged_by_axis(shard, axes, combine):
    for axis in axes:
        pieces = gathered_once(shard, axis)
        shard = jax.tree.map(lambda part: part[0], pieces)
        for k in range(1, lax.axis_size(axis)):
            shard = combine(shard, jax.tree.map(lambda part: part[k], pieces))
    return shard


def finish(token_lp, slot, prompt_len, ref_means):
    seq_count = slot.shape[0]
    per_seq = token_lp.reshape(seq_count, -1)
    seq_width = per_seq.shape[1]
    position = jnp.arange(seq_width, dtype=jnp.int32)[None, :]
    in_reply = position >= prompt_len[:, None]
    reply_len = (seq_width - prompt_len).astype(jnp.float32)
    seq_means = jnp.sum(jnp.where(in_reply, per_seq, jnp.float32(0.0)), axis=1) / reply_len
    advantage = seq_means - ref_means
    polarity = jnp.where(slot % 2 == 0, jnp.float32(1.0), jnp.float32(-1.0))
    n_pairs = seq_count // 2
    onehot = slot[:, None] // 2 == jnp.arange(n_pairs, dtype=jnp.int32)[None, :]
    signed = (polarity * advantage)[:, None]
    margins = beta_scale * jnp.sum(jnp.where(onehot, signed, jnp.float32(0.0)), axis=0)
    pair_loss = jnp.mean(jax.nn.softplus(-margins))
    return (margins, pair_loss)


def logit_stats(logits, row_targets, col_start):
    row_max = jnp.max(logits, axis=1)
    row_sum = jnp.sum(jnp.exp(logits - row_max[:, None]), axis=1)
    local_ids = row_targets - col_start
    columns = jnp.arange(logits.shape[1], dtype=jnp.int32)[None, :]
    row_target = jnp.sum(jnp.where(columns == local_ids[:, None], logits, jnp.float32(0.0)), axis=1)
    return (row_max, row_sum, row_target)


def combine(first, second):
    max_a, sum_a, target_a = first
    max_b, sum_b, target_b = second
    joined = jnp.maximum(max_a, max_b)
    summed = sum_a * jnp.exp(max_a - joined) + sum_b * jnp.exp(max_b - joined)
    return (joined, summed, target_a + target_b)


def body(hidden, weight, targets, slot, prompt_len, ref_means):
    tok_rows = hidden.shape[0]
    vocab_cols = weight.shape[1]
    col_start = (lax.axis_index(VOC) * lax.axis_size(TOK) + lax.axis_index(TOK)) * vocab_cols
    all_rows = collect(hidden, TOK, 0)
    full_rows = lax.all_gather(all_rows, VOC, axis=1, tiled=True)
    logits = jnp.dot(full_rows, weight, preferred_element_type=jnp.float32)
    row_max, row_sum, row_target = logit_stats(logits, targets, col_start)
    row_max, row_sum, row_target = merged_by_axis((row_max, row_sum, row_target), VOC_TOK, combine)
    token_lp = row_target - (row_max + jnp.log(row_sum))
    own_rows = lax.dynamic_slice_in_dim(token_lp, lax.axis_index(TOK) * tok_rows, tok_rows, 0)
    margins, pair_loss = finish(token_lp, slot, prompt_len, ref_means)
    return (own_rows, margins, pair_loss)


def solution(mesh):
    split = Mesh(mesh.devices.reshape(4, 4, 4, 2), ("tok_0", "tok_1", "voc_0", "voc_1"))
    in_specs = (P(TOK, VOC), P(None, VOC_TOK), P(), P(), P(), P())
    out_specs = (P(TOK), P(), P())
    return jax.shard_map(body, mesh=split, in_specs=in_specs, out_specs=out_specs, check_vma=False)
```

profile of v0, /device:TPU:0, one launch (start us, length us, event | category | flops | bytes accessed | tf_op | source)
XLA Modules:
  0.0 213.2 jit_solution(12821167383170841157)
XLA Ops:
  7.2 0.0 all-gather.10.cloned.1.call-start
  7.2 1.2 broadcast_in_dim.39
  8.5 33.3 %all_to_all.5 = bf16[16,128,448]{1,2,0:T(8,128)(2,1)S(1)} all-to-all(bf16[16,128,448]{1,2,0:T(8,128)(2,1)S(1)} %broadcast_in_dim.39), channel_id=1, replica_groups=mesh['tok_0'=4,'tok_1'=4,'voc_0'=4,'voc_1'=2] {'tok_0','tok_1'}, dimensions={0} | all-to-all | bytes 3670016 | tf_op jit(solution)/shard_map/all_to_all | solution.py:17
  41.8 1.5 copy_bitcast_fusion
  43.3 0.0 all-gather.10.cloned.1.call-update
  43.3 0.7 and_select_fusion.1
  44.0 0.7 broadcast_subtract_fusion
  44.7 73.1 %all-gather.10.cloned.1.call-done = bf16[2048,3584]{0,1:T(8,128)(2,1)} async-done(((bf16[2048,448]{0,1:T(8,128)(2,1)}), bf16[2048,3584]{0,1:T(8,128)(2,1)}) %all-gather.10.cloned.1.call-update) | async-done | bytes 14680080 | tf_op jit(solution)/shard_map/all_gather | solution.py:97
  117.8 37.4 %fusion.46 = (f32[2048]{0:T(1024)S(1)}, f32[2048,2000]{0,1:T(8,128)}) fusion(bf16[3584,2000]{0,1:T(8,128)(2,1)} %param.7, bf16[2048,3584]{0,1:T(8,128)(2,1)} %all-gather.10.cloned.1.call-done), kind=kOutput, calls=%fused_computation.105 | convolution fusion | flops 29364221952 | bytes 45408256 | tf_op jit(solution)/shard_map/dot_general | solution.py:98
  155.1 0.0 copy-start
  155.1 0.0 copy-start.1
  155.1 0.0 copy-start.2
  155.2 8.1 %exponential_reduce_fusion = (f32[2048]{0:T(1024)S(1)}, f32[2048]{0:T(1024)S(1)}) fusion(f32[2048,2000]{0,1:T(8,128)} %get-tuple-element.28, f32[2048]{0:T(1024)S(1)} %get-tuple-element.27, s32[2048]{0:T(1024)S(1)} %broadcast_subtract_fusion), kind=kLoop, calls=%fused_computation.2 | loop fusion | flops 20475904 | bytes 16416768 | tf_op jit(solution)/shard_map/reduce_sum | solution.py:77
  163.3 12.0 %all-gather.4 = f32[4,3,2048]{2,1,0:T(4,128)S(1)} all-gather(f32[1,3,2048]{2,1,0:T(4,128)S(1)} %maximum_bitcast_fusion), channel_id=2, replica_groups=mesh['tok_0'=4,'tok_1'=4,'voc_0'=4,'voc_1'=2] {'voc_0'}, dimensions={0}, use_global_device_ids=true | all-gather | bytes 122880 | tf_op jit(solution)/shard_map/all_gather | solution.py:39
  175.3 0.1 fusion.16
  175.4 1.9 all-gather.5
  177.4 12.3 %all-gather.6 = f32[4,3,2048]{2,1,0:T(4,128)S(1)} all-gather(f32[1,3,2048]{2,1,0:T(4,128)S(1)} %maximum_bitcast_fusion.2), channel_id=4, replica_groups=mesh['tok_0'=4,'tok_1'=4,'voc_0'=4,'voc_1'=2] {'tok_0'}, dimensions={0}, use_global_device_ids=true | all-gather | bytes 122880 | tf_op jit(solution)/shard_map/all_gather | solution.py:39
  189.8 0.1 fusion.2
  189.9 12.5 %all-gather.7 = f32[4,3,2048]{2,1,0:T(4,128)S(1)} all-gather(f32[1,3,2048]{2,1,0:T(4,128)S(1)} %maximum_bitcast_fusion.3), channel_id=5, replica_groups=mesh['tok_0'=4,'tok_1'=4,'voc_0'=4,'voc_1'=2] {'tok_1'}, dimensions={0}, use_global_device_ids=true | all-gather | bytes 122880 | tf_op jit(solution)/shard_map/all_gather | solution.py:39
  202.4 0.1 fusion.45
  202.5 0.0 copy-done
  202.5 0.2 select_reduce_fusion.1
  202.7 0.0 copy-done.1
  202.7 0.0 copy-done.2
  202.7 0.1 select_reduce_fusion.2
  202.8 1.1 fusion.38
  204.6 0.6 dynamic-slice_subtract_fusion
  (12 shorter events, 0.3 us)
Async XLA Ops:
  7.2 110.6 %all-gather.10.cloned.1.call-start = ((), (), s32[]{:S(2)}) async-start(), calls=%async_computation.1 | async-start | bytes 16515072 | tf_op jit(solution)/shard_map/all_gather | solution.py:97
  155.1 47.3 %copy-start = (s32[16]{0:T(128)S(1)}, s32[16]{0:T(128)}, u32[]{:S(2)}) copy-start(s32[16]{0:T(128)} %param.10) | copy-start | bytes 196
  155.1 47.5 %copy-start.1 = (f32[16]{0:T(128)S(1)}, f32[16]{0:T(128)}, u32[]{:S(2)}) copy-start(f32[16]{0:T(128)} %param.11) | copy-start | bytes 196
  155.1 47.5 %copy-start.2 = (s32[16]{0:T(128)S(1)}, s32[16]{0:T(128)}, u32[]{:S(2)}) copy-start(s32[16]{0:T(128)} %param.9) | copy-start | bytes 196
Sparse Core Ops, SparseCore 0:
  43.4 74.2 all-gather.9
where the time goes:
time: 213 us
  waiting for transfers between devices  73.1 us (34%)
  blocking collectives  71.9 us (34%)
  matrix products  37.4 us (18%)
  between operations  15.9 us (7%)
  other arithmetic  12 us (6%)
  local copies, waits for them, and re-layouts  2.78 us (1%)
    all_gather x1, waiting for transfers between devices, body(): full_rows = lax.all_gather(all_rows, VOC, axis=1, tiled=True)  73.1 us
    all_gather x4, blocking collectives, gathered_once(): both, at, found = (lax.all_gather(jnp.concatenate(lines), axis), 0, {})  38.7 us
    dot_general x1, matrix products, body(): logits = jnp.dot(full_rows, weight, preferred_element_type=jnp.float32)  37.4 us
    all_to_all x1, blocking collectives, sent_to_all(): return lax.all_to_all(copies, axis, split_axis=0, concat_axis=0, tiled=True)  33.3 us
    reduce_sum x1, other arithmetic, logit_stats(): row_sum = jnp.sum(jnp.exp(logits - row_max[:, None]), axis=1)  8.08 us
  transfers between devices with their start and end apart: 1, of which 1 were waited for; matrix products, arithmetic and copies ran while one was open for 1% of the time, Pallas kernels for 0%

commit v1 on v0

v1 whole, which is shorter than its diff:
```python
import functools

import jax
import jax.numpy as jnp
from jax import lax
from jax.experimental import pallas as pl
from jax.experimental.pallas import tpu as pltpu
from jax.sharding import Mesh
from jax.sharding import PartitionSpec as P

Y, Z, X, C = "tok_0", "tok_1", "voc_0", "voc_1"
VOC = (X, C)
TOK = (Y, Z)
VOC_TOK = (X, C, Y, Z)
CHIPS = (Y, Z, X)
EVERY = (Y, Z, X, C)

RING = 4
SWAP = [(0, 1), (1, 0)]
PLACE = (0, 2, 3, 1)
BLOCK_ROWS = 400

beta_scale = 2.0


def ring_pairs(step):
    return [(i, (i + step) % RING) for i in range(RING)]


def crossed_pairs(first, step):
    pairs = []
    for y in range(4):
        for z in range(4):
            for x in range(4):
                for c in range(2):
                    along_z = (c == 0) == first
                    y2, z2 = (y, (z + step) % RING) if along_z else ((y + step) % RING, z)
                    pairs.append((((y * 4 + z) * 4 + x) * 2 + c, ((y2 * 4 + z2) * 4 + x) * 2 + c))
    return pairs


def shifted(block, first, step):
    return lax.ppermute(block, EVERY, crossed_pairs(first, step))


def finish(per_seq, slot, prompt_len, ref_means):
    seq_count, seq_width = per_seq.shape
    position = jnp.arange(seq_width, dtype=jnp.int32)[None, :]
    in_reply = position >= prompt_len[:, None]
    reply_len = (seq_width - prompt_len).astype(jnp.float32)
    seq_means = jnp.sum(jnp.where(in_reply, per_seq, jnp.float32(0.0)), axis=1) / reply_len
    advantage = seq_means - ref_means
    polarity = jnp.where(slot % 2 == 0, jnp.float32(1.0), jnp.float32(-1.0))
    n_pairs = seq_count // 2
    onehot = slot[:, None] // 2 == jnp.arange(n_pairs, dtype=jnp.int32)[None, :]
    signed = (polarity * advantage)[:, None]
    margins = beta_scale * jnp.sum(jnp.where(onehot, signed, jnp.float32(0.0)), axis=0)
    pair_loss = jnp.mean(jax.nn.softplus(-margins))
    return (margins, pair_loss)


def stats_kernel(local_ids, *refs, counts):
    n_in = len(counts)
    parts = refs[:n_in]
    w_own, w_other, out, rows, top, total, picked = refs[n_in:]
    width = rows.shape[1]
    step = pl.program_id(0)

    @pl.when(step == 0)
    def _():
        pieces = [(ref, k) for ref, n in zip(parts, counts) for k in range(n)]
        for p in range(len(pieces) // 2):
            (ref_a, ka), (ref_b, kb) = pieces[2 * p], pieces[2 * p + 1]
            lanes = slice(p * 128, (p + 1) * 128)
            for x in range(4):
                a = ref_a[ka * 1792 + x * 448 : ka * 1792 + (x + 1) * 448, :]
                b = ref_b[kb * 1792 + x * 448 : kb * 1792 + (x + 1) * 448, :]
                rows[2 * x * 448 : (2 * x + 1) * 448, lanes] = jnp.concatenate([a[:, :64], b[:, :64]], 1)
                rows[(2 * x + 1) * 448 : (2 * x + 2) * 448, lanes] = jnp.concatenate([a[:, 64:], b[:, 64:]], 1)
        top[...] = jnp.full_like(top, -jnp.inf)
        total[...] = jnp.zeros_like(total)
        picked[...] = jnp.zeros_like(picked)

    for k, w in enumerate((w_own, w_other)):
        logits = jnp.dot(w[...], rows[...], preferred_element_type=jnp.float32)
        tiles = logits.reshape(BLOCK_ROWS // 8, 8, width)
        before = top[...]
        now = jnp.maximum(before, jnp.max(tiles, 0))
        total[...] = total[...] * jnp.exp(before - now) + jnp.sum(jnp.exp(tiles - now[None]), 0)
        top[...] = now
        ids = lax.broadcasted_iota(jnp.int32, (BLOCK_ROWS, width), 0)
        hit = ids == local_ids[k : k + 1, :] - step * BLOCK_ROWS
        picked[...] += jnp.sum(jnp.where(hit, logits, 0.0).reshape(BLOCK_ROWS // 8, 8, width), 0)

    @pl.when(step == pl.num_programs(0) - 1)
    def _():
        peak = jnp.max(top[...], 0, keepdims=True)
        mass = jnp.sum(total[...] * jnp.exp(top[...] - peak), 0, keepdims=True)
        out[0:1, :] = peak + jnp.log(mass)
        out[1:2, :] = jnp.sum(picked[...], 0, keepdims=True)


def chunk_stats(w_own, w_other, local_ids, *parts):
    counts = tuple(part.shape[0] // 1792 for part in parts)
    width = 64 * sum(counts)
    vocab, depth = w_own.shape
    whole = lambda shape: pl.BlockSpec(shape, lambda i: (0, 0))
    once = lambda shape: pl.BlockSpec(shape, lambda i: (0, 0), pipeline_mode=pl.Buffered(1))
    tile = pl.BlockSpec((BLOCK_ROWS, depth), lambda i: (i, 0))
    return pl.pallas_call(
        functools.partial(stats_kernel, counts=counts),
        grid=(vocab // BLOCK_ROWS,),
        in_specs=[whole((2, width))] + [once(part.shape) for part in parts] + [tile, tile],
        out_specs=whole((2, width)),
        out_shape=jax.ShapeDtypeStruct((2, width), jnp.float32),
        scratch_shapes=[pltpu.VMEM((depth, width), jnp.bfloat16)] + [pltpu.VMEM((8, width), jnp.float32)] * 3,
        compiler_params=pltpu.CompilerParams(vmem_limit_bytes=40 * 2**20),
        cost_estimate=pl.CostEstimate(
            flops=4 * width * vocab * depth, bytes_accessed=4 * vocab * depth, transcendentals=2 * vocab * width
        ),
    )(local_ids, *parts, pltpu.with_memory_space_constraint(w_own, pltpu.HBM), pltpu.with_memory_space_constraint(w_other, pltpu.HBM))


def body(hidden, weight, targets, slot, prompt_len, ref_means):
    y, z, x, c = (lax.axis_index(axis) for axis in EVERY)
    vocab_cols = weight.shape[1]
    w_own = weight.T
    mine = hidden.T

    theirs = lax.ppermute(mine, C, SWAP)
    low = jnp.concatenate([mine[:, :64], theirs[:, :64]], 1)
    high = jnp.concatenate([theirs[:, 64:], mine[:, 64:]], 1)
    half = jnp.where(c == 0, low, high)
    behind, ahead, across = (lax.ppermute(half, X, ring_pairs(s)) for s in (1, 3, 2))
    turned = jnp.concatenate([half, ahead, across, behind, half, ahead, across], 0)
    own = lax.dynamic_slice_in_dim(turned, lax.rem(4 - x, 4) * 448, 1792, 0)

    w_other = lax.ppermute(w_own, C, SWAP)

    group = jnp.arange(16, dtype=jnp.int32)
    offset = jnp.array([0, 3, 1, 2], jnp.int32)
    off_a, off_b = offset[group % 4], offset[group // 4]
    off_y, off_z = jnp.where(c == 0, off_b, off_a), jnp.where(c == 0, off_a, off_b)
    source = (y + off_y) % 4 * 4 + (z + off_z) % 4
    ids = jnp.take(targets.reshape(32, 64), source * 2 + c, axis=0).reshape(1, 1024)
    start = lambda core: (((x * 2 + core) * 4 + y) * 4 + z) * vocab_cols
    local_ids = jnp.concatenate([ids - start(c), ids - start(1 - c)], 0)

    a_behind, a_ahead = shifted(own, True, 1), shifted(own, True, 3)
    a_across = [shifted(a_behind[:896], True, 1), shifted(a_ahead[896:], True, 3)]
    chunk = jnp.concatenate([own, a_behind, a_ahead, *a_across], 0)
    b_behind, b_ahead = shifted(chunk, False, 1), shifted(chunk, False, 3)
    first = chunk_stats(w_own, w_other, local_ids[:, :256], chunk)
    b_behind, b_ahead, first = lax.optimization_barrier((b_behind, b_ahead, first))
    b_across = [shifted(b_behind[:3584], False, 1), shifted(b_ahead[3584:], False, 3)]

    second = chunk_stats(w_own, w_other, local_ids[:, 256:768], b_behind, b_ahead)
    b_across = lax.optimization_barrier((b_across, second))
    b_across, second = b_across
    third = chunk_stats(w_own, w_other, local_ids[:, 768:], *b_across)
    stats = jnp.concatenate([first, second, third], 1).reshape(2, 16, 64)

    group_y, group_z = (group // 4 - y) % 4, (group % 4 - z) % 4
    place = jnp.array(PLACE, jnp.int32)
    at_a, at_b = place[jnp.where(c == 0, group_z, group_y)], place[jnp.where(c == 0, group_y, group_z)]
    stats = jnp.take(stats, at_b * 4 + at_a, axis=1).reshape(2, 1024)

    copies = jnp.broadcast_to(stats, (64, 2, 1024))
    parts = lax.all_to_all(copies, CHIPS, split_axis=0, concat_axis=0, tiled=True)
    peak = jnp.max(parts[:, 0], 0)
    mass = jnp.sum(jnp.exp(parts[:, 0] - peak), 0)
    token_lp = (jnp.sum(parts[:, 1], 0) - (peak + jnp.log(mass))).reshape(16, 64)
    other_lp = lax.ppermute(token_lp, C, SWAP)
    per_seq = jnp.where(
        c == 0, jnp.concatenate([token_lp, other_lp], 1), jnp.concatenate([other_lp, token_lp], 1)
    )
    own_rows = lax.dynamic_slice_in_dim(per_seq, y * 4 + z, 1, 0).reshape(128)
    margins, pair_loss = finish(per_seq, slot, prompt_len, ref_means)
    return (own_rows, margins, pair_loss)


def solution(mesh):
    split = Mesh(mesh.devices.reshape(4, 4, 4, 2), EVERY)
    in_specs = (P(TOK, VOC), P(None, VOC_TOK), P(), P(), P(), P())
    out_specs = (P(TOK), P(), P())
    return jax.shard_map(body, mesh=split, in_specs=in_specs, out_specs=out_specs, check_vma=False)
```

time: 213 us -> 134 us (0.63)
  blocking collectives: 71.9 us -> 15.9 us
  Pallas kernels: 0 us -> 50 us
  waiting for transfers between devices: 73.1 us -> 31.9 us
  matrix products: 37.4 us -> 0 us
  starting transfers between devices: 0.04 us -> 20.2 us
  between operations: 15.9 us -> 2.86 us
  other arithmetic: 12 us -> 2.4 us
  local copies, waits for them, and re-layouts: 2.78 us -> 9.15 us
    all_gather x1 -> x0, waiting for transfers between devices: 73.1 us -> none  [body(): full_rows = lax.all_gather(all_rows, VOC, axis=1, tiled=True)]
    pallas_call x0 -> x3, Pallas kernels: none -> 50 us  [chunk_stats(): pl.pallas_call(functools.partial(stats_kernel, counts=counts), grid=(voca...]
    all_gather x4 -> x0, blocking collectives: 38.7 us -> none  [gathered_once(): both, at, found = (lax.all_gather(jnp.concatenate(lines), axis), 0, {})]
    dot_general x1 -> x0, matrix products: 37.4 us -> none  [body(): logits = jnp.dot(full_rows, weight, preferred_element_type=jnp.float32)]
    ppermute x0 -> x14, waiting for transfers between devices: none -> 31.9 us  [the longest x8 19.6 us: shifted(): return lax.ppermute(block, EVERY, crossed_pairs(first, step))]
    ppermute x0 -> x14, starting transfers between devices: none -> 20.2 us  [the longest x8 14.3 us: shifted(): return lax.ppermute(block, EVERY, crossed_pairs(first, step))]
    all_to_all x1, blocking collectives: 33.3 us -> 15.9 us  [body(): lax.all_to_all(copies, CHIPS, split_axis=0, concat_axis=0, tiled=True)]
    reduce_sum x1, other arithmetic: 8.08 us -> 0.07 us  [body(): mass = jnp.sum(jnp.exp(parts[:, 0] - peak), 0)]
  transfers between devices with their start and end apart: 1 -> 14, of which waited for: 1 -> 9; matrix products, arithmetic and copies ran while one was open for 1% -> 4% of each run, Pallas kernels for 0% -> 27%
where the time goes in v1:
time: 134 us; the launch traced here: 132 us
  Pallas kernels  50 us (37%)
  waiting for transfers between devices  31.9 us (24%)
  starting transfers between devices  20.2 us (15%)
  blocking collectives  15.9 us (12%)
  local copies, waits for them, and re-layouts  9.15 us (7%)
  between operations  2.86 us (2%)
  other arithmetic  2.4 us (2%)
    pallas_call x3, Pallas kernels, chunk_stats(): pl.pallas_call(functools.partial(stats_kernel, counts=counts), grid=(voca...  50 us
    ppermute x8, waiting for transfers between devices, shifted(): return lax.ppermute(block, EVERY, crossed_pairs(first, step))  19.6 us
    all_to_all x1, blocking collectives, body(): lax.all_to_all(copies, CHIPS, split_axis=0, concat_axis=0, tiled=True)  15.9 us
    ppermute x8, starting transfers between devices, shifted(): return lax.ppermute(block, EVERY, crossed_pairs(first, step))  14.3 us
    ppermute x3, waiting for transfers between devices, body(): lax.ppermute(half, X, ring_pairs(s))  6.45 us
    ppermute x3, starting transfers between devices, body(): lax.ppermute(half, X, ring_pairs(s))  5.28 us
    ppermute x1, waiting for transfers between devices, body(): theirs = lax.ppermute(mine, C, SWAP)  4.75 us
  transfers between devices with their start and end apart: 14, of which 9 were waited for; matrix products, arithmetic and copies ran while one was open for 4% of the time, Pallas kernels for 27%

profile of v1, /device:TPU:0, one launch (start us, length us, event | category | flops | bytes accessed | tf_op | source)
XLA Modules:
  0.0 132.4 jit_solution(3608002042595959817)
XLA Ops:
  0.7 0.5 collective-permute-start
  1.2 1.1 fusion.25
  2.3 4.7 %collective-permute-done = bf16[448,128]{1,0:T(8,128)(2,1)S(1)} collective-permute-done((bf16[448,128]{1,0:T(8,128)(2,1)}, bf16[448,128]{1,0:T(8,128)(2,1)S(1)}, u32[]{:S(2)}, u32[]{:S(2)}) %collective-permute-start) | collective-permute-done | bytes 114720 | tf_op jit(solution)/shard_map/ppermute | solution.py:130
  7.3 2.9 %collective-permute-start.1 = (bf16[448,128]{1,0:T(8,128)(2,1)S(1)}, bf16[448,128]{1,0:T(8,128)(2,1)S(1)}, u32[]{:S(2)}, u32[]{:S(2)}) collective-permute-start(bf16[448,128]{1,0:T(8,128)(2,1)S(1)} %get-tuple-element.24), channel_id=1, source_target_pairs={{0,6},{2,0},{4,2},{6,4},{1,7},{3,1},{5,3},{7,5},{8,14},{10,8},{12,... | collective-permute-start | bytes 344072 | tf_op jit(solution)/shard_map/ppermute | solution.py:134
  10.3 2.3 %collective-permute-start.2 = (bf16[448,128]{1,0:T(8,128)(2,1)S(1)}, bf16[448,128]{1,0:T(8,128)(2,1)S(1)}, u32[]{:S(2)}, u32[]{:S(2)}) collective-permute-start(bf16[448,128]{1,0:T(8,128)(2,1)S(1)} %get-tuple-element.24), channel_id=1, source_target_pairs={{0,4},{2,6},{4,0},{6,2},{1,5},{3,7},{5,1},{7,3},{8,12},{10,14},{12... | collective-permute-start | bytes 344072 | tf_op jit(solution)/shard_map/ppermute | solution.py:134
  12.6 0.6 collective-permute-done.1
  13.2 5.1 %collective-permute-done.2 = bf16[448,128]{1,0:T(8,128)(2,1)S(1)} collective-permute-done((bf16[448,128]{1,0:T(8,128)(2,1)S(1)}, bf16[448,128]{1,0:T(8,128)(2,1)S(1)}, u32[]{:S(2)}, u32[]{:S(2)}) %collective-permute-start.2) | collective-permute-done | bytes 114720 | tf_op jit(solution)/shard_map/ppermute | solution.py:134
  18.3 0.8 collective-permute-done.3
  19.3 4.1 %collective-permute-start.5 = (bf16[1792,128]{1,0:T(8,128)(2,1)S(1)}, bf16[1792,128]{1,0:T(8,128)(2,1)S(1)}, u32[]{:S(2)}, u32[]{:S(2)}) collective-permute-start(bf16[1792,128]{1,0:T(8,128)(2,1)S(1)} %get-tuple-element.22), channel_id=1, source_target_pairs={{0,24},{1,97},{2,26},{3,99},{4,28},{5,101},{6,30},{7,103},{8,0},{9... | collective-permute-start | bytes 1376264 | tf_op jit(solution)/shard_map/ppermute | solution.py:43
  23.4 0.7 gather_fusion.2
  24.1 0.7 gather_fusion.3
  24.8 0.7 gather_fusion
  25.5 0.7 gather_fusion.1
  26.2 3.2 %collective-permute-done.5 = bf16[1792,128]{1,0:T(8,128)(2,1)S(1)} collective-permute-done((bf16[1792,128]{1,0:T(8,128)(2,1)S(1)}, bf16[1792,128]{1,0:T(8,128)(2,1)S(1)}, u32[]{:S(2)}, u32[]{:S(2)}) %collective-permute-start.5) | collective-permute-done | bytes 458784 | tf_op jit(solution)/shard_map/ppermute | solution.py:43
  29.4 3.8 %collective-permute-start.7 = (bf16[896,128]{1,0:T(8,128)(2,1)S(1)}, bf16[896,128]{1,0:T(8,128)(2,1)S(1)}, u32[]{:S(2)}, u32[]{:S(2)}) collective-permute-start(bf16[896,128]{1,0:T(8,128)(2,1)S(1)} %slice.70), channel_id=1, source_target_pairs={{0,24},{1,97},{2,26},{3,99},{4,28},{5,101},{6,30},{7,103},{8,0},{9... | collective-permute-start | bytes 688136 | tf_op jit(solution)/shard_map/ppermute | solution.py:43
  33.4 7.1 %collective-permute-done.6 = bf16[896,128]{1,0:T(8,128)(2,1)S(1)} collective-permute-done((bf16[896,128]{1,0:T(8,128)(2,1)S(1)}, bf16[896,128]{1,0:T(8,128)(2,1)S(1)}, u32[]{:S(2)}, u32[]{:S(2)}) %collective-permute-start.6) | collective-permute-done | bytes 229408 | tf_op jit(solution)/shard_map/ppermute | solution.py:43
  40.6 3.1 %collective-permute-start.9 = (bf16[7168,128]{1,0:T(8,128)(2,1)S(1)}, bf16[7168,128]{1,0:T(8,128)(2,1)}, u32[]{:S(2)}, u32[]{:S(2)}) collective-permute-start(bf16[7168,128]{1,0:T(8,128)(2,1)S(1)} %constant_dynamic-update-slice_fusion.7.refs_0_), channel_id=1, source_target_pairs={{0,96},{1,25},{2,98},{3,27},{4,100},{5,29},{6,102},{7,31},{8,104},... | collective-permute-start | bytes 5505032 | tf_op jit(solution)/shard_map/ppermute | solution.py:43
  44.0 0.6 gather_fusion.4
  44.9 14.1 %shard_map.103 = f32[2,256]{1,0:T(2,128)S(1)} custom-call(s32[2,256]{1,0:T(2,128)S(1)} %get-tuple-element.35.local_ids, bf16[7168,128]{1,0:T(8,128)(2,1)S(1)} %constant_dynamic-update-slice_fusion.7.refs_0_, bf16[2000,3584]{1,0:T(8,128)(2,1)} %bitcast.34, bf16[2000,3584]{1,0:T(8,128)(2,1)} %collective-permute-done.10.refs_2_.refs_3_), custom_call_target="tpu_custom_call" | custom-call | flops 7340032000 | bytes 28672000 | tf_op jit(solution)/shard_map/pallas_call | solution.py:110
  58.9 5.5 %collective-permute-done.9.refs_1_ = bf16[7168,128]{1,0:T(8,128)(2,1)} collective-permute-done((bf16[7168,128]{1,0:T(8,128)(2,1)S(1)}, bf16[7168,128]{1,0:T(8,128)(2,1)}, u32[]{:S(2)}, u32[]{:S(2)}) %collective-permute-start.9) | collective-permute-done | bytes 1835040 | tf_op jit(solution)/shard_map/ppermute | solution.py:43
  64.4 3.8 %collective-permute-done.8.refs_0_ = bf16[7168,128]{1,0:T(8,128)(2,1)} collective-permute-done((bf16[7168,128]{1,0:T(8,128)(2,1)S(1)}, bf16[7168,128]{1,0:T(8,128)(2,1)}, u32[]{:S(2)}, u32[]{:S(2)}) %collective-permute-start.8) | collective-permute-done | bytes 1835040 | tf_op jit(solution)/shard_map/ppermute | solution.py:43
  68.2 1.2 slice.48
  69.5 1.2 slice.47
  70.8 3.2 %collective-permute-start.12 = (bf16[3584,128]{1,0:T(8,128)(2,1)S(1)}, bf16[3584,128]{1,0:T(8,128)(2,1)S(1)}, u32[]{:S(2)}, u32[]{:S(2)}) collective-permute-start(bf16[3584,128]{1,0:T(8,128)(2,1)S(1)} %slice.48), channel_id=1, source_target_pairs={{0,96},{1,25},{2,98},{3,27},{4,100},{5,29},{6,102},{7,31},{8,104},... | collective-permute-start | bytes 2752520 | tf_op jit(solution)/shard_map/ppermute | solution.py:43
  74.0 21.8 %shard_map.104 = f32[2,512]{1,0:T(2,128)S(1)} custom-call(s32[2,512]{1,0:T(2,128)S(1)} %fusion.2.local_ids, bf16[7168,128]{1,0:T(8,128)(2,1)} %collective-permute-done.8.refs_0_, bf16[7168,128]{1,0:T(8,128)(2,1)} %collective-permute-done.9.refs_1_, bf16[2000,3584]{1,0:T(8,128)(2,1)} %bitcast.35, bf16[2000,3584]{1,0:T(8,128)(2,1)} %collective-permute-done.10.refs_2_.refs_3_), custom_call_target="tpu_custom_call" | custom-call | flops 14680064000 | bytes 28672000 | tf_op jit(solution)/shard_map/pallas_call | solution.py:110
  95.9 14.1 %shard_map.105 = f32[2,256]{1,0:T(2,128)S(1)} custom-call(s32[2,256]{1,0:T(2,128)S(1)} %get-tuple-element.36.local_ids, bf16[3584,128]{1,0:T(8,128)(2,1)S(1)} %collective-permute-done.11.refs_0_, bf16[3584,128]{1,0:T(8,128)(2,1)S(1)} %collective-permute-done.12.refs_1_, bf16[2000,3584]{1,0:T(8,128)(2,1)} %bitcast.36, ...), custom_call_target="tpu_custom_call" | custom-call | flops 7340032000 | bytes 28672000 | tf_op jit(solution)/shard_map/pallas_call | solution.py:110
  110.1 0.6 gather_fusion.5
  110.9 15.9 %all_to_all.5 = f32[64,2,1024]{2,1,0:T(2,128)S(1)} all-to-all(f32[64,2,1024]{2,1,0:T(2,128)S(1)} %broadcast_in_dim.67), channel_id=1, replica_groups=mesh['tok_0'=4,'tok_1'=4,'voc_0'=4,'voc_1'=2] {'tok_0','tok_1','voc_0'}, dimensions={0} | all-to-all | bytes 1048576 | tf_op jit(solution)/shard_map/all_to_all | solution.py:169
  126.8 0.5 slice_reduce_fusion.1
  127.5 1.1 collective-permute-done.13
  129.0 1.1 fusion.20
  130.1 0.5 dynamic-slice_bitcast_fusion
  (74 shorter events, 2.5 us)
Async XLA Ops:
  0.6 44.2 %collective-permute-start.10 = (bf16[2000,3584]{1,0:T(8,128)(2,1)}, bf16[2000,3584]{1,0:T(8,128)(2,1)}, u32[]{:S(2)}, u32[]{:S(2)}) collective-permute-start(bf16[2000,3584]{1,0:T(8,128)(2,1)} %bitcast.33), channel_id=1, source_target_pairs={{0,1},{1,0},{2,3},{3,2},{4,5},{5,4},{6,7},{7,6},{8,9},{9,8},{10,11... | collective-permute-start | bytes 43008008 | tf_op jit(solution)/shard_map/ppermute | solution.py:138
  0.7 6.3 %collective-permute-start = (bf16[448,128]{1,0:T(8,128)(2,1)}, bf16[448,128]{1,0:T(8,128)(2,1)S(1)}, u32[]{:S(2)}, u32[]{:S(2)}) collective-permute-start(bf16[448,128]{1,0:T(8,128)(2,1)} %bitcast.37), channel_id=1, source_target_pairs={{0,1},{1,0},{2,3},{3,2},{4,5},{5,4},{6,7},{7,6},{8,9},{9,8},{10,11... | collective-permute-start | bytes 344072 | tf_op jit(solution)/shard_map/ppermute | solution.py:130
  7.2 16.3 %copy-start.1 = (s32[4]{0:T(128)S(1)}, s32[4]{0:T(128)}, u32[]{:S(2)}) copy-start(s32[4]{0:T(128)} %constant.163.clone) | copy-start | bytes 52
  7.3 5.9 %collective-permute-start.1 = (bf16[448,128]{1,0:T(8,128)(2,1)S(1)}, bf16[448,128]{1,0:T(8,128)(2,1)S(1)}, u32[]{:S(2)}, u32[]{:S(2)}) collective-permute-start(bf16[448,128]{1,0:T(8,128)(2,1)S(1)} %get-tuple-element.24), channel_id=1, source_target_pairs={{0,6},{2,0},{4,2},{6,4},{1,7},{3,1},{5,3},{7,5},{8,14},{10,8},{12,... | collective-permute-start | bytes 344072 | tf_op jit(solution)/shard_map/ppermute | solution.py:134
  10.3 8.9 %collective-permute-start.3 = (bf16[448,128]{1,0:T(8,128)(2,1)S(1)}, bf16[448,128]{1,0:T(8,128)(2,1)S(1)}, u32[]{:S(2)}, u32[]{:S(2)}) collective-permute-start(bf16[448,128]{1,0:T(8,128)(2,1)S(1)} %get-tuple-element.24), channel_id=1, source_target_pairs={{0,2},{2,4},{4,6},{6,0},{1,3},{3,5},{5,7},{7,1},{8,10},{10,12},{12... | collective-permute-start | bytes 344072 | tf_op jit(solution)/shard_map/ppermute | solution.py:134
  10.3 7.9 %collective-permute-start.2 = (bf16[448,128]{1,0:T(8,128)(2,1)S(1)}, bf16[448,128]{1,0:T(8,128)(2,1)S(1)}, u32[]{:S(2)}, u32[]{:S(2)}) collective-permute-start(bf16[448,128]{1,0:T(8,128)(2,1)S(1)} %get-tuple-element.24), channel_id=1, source_target_pairs={{0,4},{2,6},{4,0},{6,2},{1,5},{3,7},{5,1},{7,3},{8,12},{10,14},{12... | collective-permute-start | bytes 344072 | tf_op jit(solution)/shard_map/ppermute | solution.py:134
  13.2 11.6 %copy-start = (s32[4]{0:T(128)S(1)}, s32[4]{0:T(128)}, u32[]{:S(2)}) copy-start(s32[4]{0:T(128)} %constant.164.clone) | copy-start | bytes 52
  19.3 10.1 %collective-permute-start.5 = (bf16[1792,128]{1,0:T(8,128)(2,1)S(1)}, bf16[1792,128]{1,0:T(8,128)(2,1)S(1)}, u32[]{:S(2)}, u32[]{:S(2)}) collective-permute-start(bf16[1792,128]{1,0:T(8,128)(2,1)S(1)} %get-tuple-element.22), channel_id=1, source_target_pairs={{0,24},{1,97},{2,26},{3,99},{4,28},{5,101},{6,30},{7,103},{8,0},{9... | collective-permute-start | bytes 1376264 | tf_op jit(solution)/shard_map/ppermute | solution.py:43
  23.4 9.8 %collective-permute-start.4 = (bf16[1792,128]{1,0:T(8,128)(2,1)S(1)}, bf16[1792,128]{1,0:T(8,128)(2,1)S(1)}, u32[]{:S(2)}, u32[]{:S(2)}) collective-permute-start(bf16[1792,128]{1,0:T(8,128)(2,1)S(1)} %get-tuple-element.22), channel_id=1, source_target_pairs={{0,8},{1,33},{2,10},{3,35},{4,12},{5,37},{6,14},{7,39},{8,16},{9,4... | collective-permute-start | bytes 1376264 | tf_op jit(solution)/shard_map/ppermute | solution.py:43
  26.2 17.7 %copy-start.2 = (s32[2048]{0:T(1024)S(1)}, s32[2048]{0:T(1024)}, u32[]{:S(2)}) copy-start(s32[2048]{0:T(1024)} %param.10) | copy-start | bytes 24580
  29.4 11.1 %collective-permute-start.7 = (bf16[896,128]{1,0:T(8,128)(2,1)S(1)}, bf16[896,128]{1,0:T(8,128)(2,1)S(1)}, u32[]{:S(2)}, u32[]{:S(2)}) collective-permute-start(bf16[896,128]{1,0:T(8,128)(2,1)S(1)} %slice.70), channel_id=1, source_target_pairs={{0,24},{1,97},{2,26},{3,99},{4,28},{5,101},{6,30},{7,103},{8,0},{9... | collective-permute-start | bytes 688136 | tf_op jit(solution)/shard_map/ppermute | solution.py:43
  33.2 7.3 %collective-permute-start.6 = (bf16[896,128]{1,0:T(8,128)(2,1)S(1)}, bf16[896,128]{1,0:T(8,128)(2,1)S(1)}, u32[]{:S(2)}, u32[]{:S(2)}) collective-permute-start(bf16[896,128]{1,0:T(8,128)(2,1)S(1)} %slice.69), channel_id=1, source_target_pairs={{0,8},{1,33},{2,10},{3,35},{4,12},{5,37},{6,14},{7,39},{8,16},{9,4... | collective-permute-start | bytes 688136 | tf_op jit(solution)/shard_map/ppermute | solution.py:43
  40.6 23.8 %collective-permute-start.9 = (bf16[7168,128]{1,0:T(8,128)(2,1)S(1)}, bf16[7168,128]{1,0:T(8,128)(2,1)}, u32[]{:S(2)}, u32[]{:S(2)}) collective-permute-start(bf16[7168,128]{1,0:T(8,128)(2,1)S(1)} %constant_dynamic-update-slice_fusion.7.refs_0_), channel_id=1, source_target_pairs={{0,96},{1,25},{2,98},{3,27},{4,100},{5,29},{6,102},{7,31},{8,104},... | collective-permute-start | bytes 5505032 | tf_op jit(solution)/shard_map/ppermute | solution.py:43
  43.7 24.5 %collective-permute-start.8 = (bf16[7168,128]{1,0:T(8,128)(2,1)S(1)}, bf16[7168,128]{1,0:T(8,128)(2,1)}, u32[]{:S(2)}, u32[]{:S(2)}) collective-permute-start(bf16[7168,128]{1,0:T(8,128)(2,1)S(1)} %constant_dynamic-update-slice_fusion.7.refs_0_), channel_id=1, source_target_pairs={{0,32},{1,9},{2,34},{3,11},{4,36},{5,13},{6,38},{7,15},{8,40},{9,1... | collective-permute-start | bytes 5505032 | tf_op jit(solution)/shard_map/ppermute | solution.py:43
  70.7 25.2 %collective-permute-start.11 = (bf16[3584,128]{1,0:T(8,128)(2,1)S(1)}, bf16[3584,128]{1,0:T(8,128)(2,1)S(1)}, u32[]{:S(2)}, u32[]{:S(2)}) collective-permute-start(bf16[3584,128]{1,0:T(8,128)(2,1)S(1)} %slice.47), channel_id=1, source_target_pairs={{0,32},{1,9},{2,34},{3,11},{4,36},{5,13},{6,38},{7,15},{8,40},{9,1... | collective-permute-start | bytes 2752520 | tf_op jit(solution)/shard_map/ppermute | solution.py:43
  70.8 25.1 %collective-permute-start.12 = (bf16[3584,128]{1,0:T(8,128)(2,1)S(1)}, bf16[3584,128]{1,0:T(8,128)(2,1)S(1)}, u32[]{:S(2)}, u32[]{:S(2)}) collective-permute-start(bf16[3584,128]{1,0:T(8,128)(2,1)S(1)} %slice.48), channel_id=1, source_target_pairs={{0,96},{1,25},{2,98},{3,27},{4,100},{5,29},{6,102},{7,31},{8,104},... | collective-permute-start | bytes 2752520 | tf_op jit(solution)/shard_map/ppermute | solution.py:43
  109.9 17.5 %copy-start.5 = (s32[16]{0:T(128)S(1)}, s32[16]{0:T(128)}, u32[]{:S(2)}) copy-start(s32[16]{0:T(128)} %param.11) | copy-start | bytes 196
  110.0 18.7 %copy-start.3 = (s32[16]{0:T(128)S(1)}, s32[16]{0:T(128)}, u32[]{:S(2)}) copy-start(s32[16]{0:T(128)} %param.12) | copy-start | bytes 196
  110.0 18.9 %copy-start.4 = (f32[16]{0:T(128)S(1)}, f32[16]{0:T(128)}, u32[]{:S(2)}) copy-start(f32[16]{0:T(128)} %param.13) | copy-start | bytes 196
  127.5 1.2 collective-permute-start.13

commit v2 on v1

v2 whole, which is shorter than its diff:
```python
import functools

import jax
import jax.numpy as jnp
import numpy as np
from jax import lax
from jax.experimental import pallas as pl
from jax.experimental.pallas import tpu as pltpu
from jax.sharding import Mesh
from jax.sharding import PartitionSpec as P

Y, Z, X, C = "tok_0", "tok_1", "voc_0", "voc_1"
VOC = (X, C)
TOK = (Y, Z)
VOC_TOK = (X, C, Y, Z)
CHIPS = (Y, Z, X)
EVERY = (Y, Z, X, C)

RING = 4
SWAP = [(0, 1), (1, 0)]
ALONG_A = np.array([0, 3, 1, 2, 0, 3, 1, 2, 1, 2, 0, 3, 0, 3, 1, 2], np.int32)
ALONG_B = np.array([0, 0, 0, 0, 3, 3, 1, 1, 3, 3, 1, 1, 2, 2, 2, 2], np.int32)
PLACE = np.zeros(16, np.int32)
PLACE[ALONG_A * 4 + ALONG_B] = np.arange(16)
ROWS = 1792
BLOCK_ROWS = 400
AHEAD = 3

beta_scale = 2.0


def ring_pairs(step):
    return [(i, (i + step) % RING) for i in range(RING)]


def crossed_pairs(first, step):
    pairs = []
    for y in range(4):
        for z in range(4):
            for x in range(4):
                for c in range(2):
                    along_z = (c == 0) == first
                    y2, z2 = (y, (z + step) % RING) if along_z else ((y + step) % RING, z)
                    pairs.append((((y * 4 + z) * 4 + x) * 2 + c, ((y2 * 4 + z2) * 4 + x) * 2 + c))
    return pairs


def shifted(block, first, step):
    return lax.ppermute(block, EVERY, crossed_pairs(first, step))


def finish(per_seq, slot, prompt_len, ref_means):
    seq_count, seq_width = per_seq.shape
    position = jnp.arange(seq_width, dtype=jnp.int32)[None, :]
    in_reply = position >= prompt_len[:, None]
    reply_len = (seq_width - prompt_len).astype(jnp.float32)
    seq_means = jnp.sum(jnp.where(in_reply, per_seq, jnp.float32(0.0)), axis=1) / reply_len
    advantage = seq_means - ref_means
    polarity = jnp.where(slot % 2 == 0, jnp.float32(1.0), jnp.float32(-1.0))
    n_pairs = seq_count // 2
    onehot = slot[:, None] // 2 == jnp.arange(n_pairs, dtype=jnp.int32)[None, :]
    signed = (polarity * advantage)[:, None]
    margins = beta_scale * jnp.sum(jnp.where(onehot, signed, jnp.float32(0.0)), axis=0)
    pair_loss = jnp.mean(jax.nn.softplus(-margins))
    return (margins, pair_loss)


def stats_kernel(local_ids, *refs, counts):
    n_in = len(counts)
    parts = refs[:n_in]
    *far, out, near, rows, top, total, picked, arrived = refs[n_in:]
    width = rows.shape[1]
    steps = near.shape[1] // BLOCK_ROWS

    def block(i):
        return pl.ds(pl.multiple_of(i * BLOCK_ROWS, BLOCK_ROWS), BLOCK_ROWS)

    def bringing(k, i):
        return pltpu.make_async_copy(far[k].at[block(i), :], near.at[k, block(i), :], arrived.at[k, i])

    for i in range(AHEAD):
        bringing(0, i).start()

    pieces = [(ref, k * ROWS) for ref, n in zip(parts, counts) for k in range(n)]
    for p in range(len(pieces) // 2):
        (ref_a, at_a), (ref_b, at_b) = pieces[2 * p], pieces[2 * p + 1]
        lanes = slice(p * 128, (p + 1) * 128)
        for x in range(4):
            a = ref_a[at_a + x * 448 : at_a + (x + 1) * 448, :]
            b = ref_b[at_b + x * 448 : at_b + (x + 1) * 448, :]
            rows[2 * x * 448 : (2 * x + 1) * 448, lanes] = jnp.concatenate([a[:, :64], b[:, :64]], 1)
            rows[(2 * x + 1) * 448 : (2 * x + 2) * 448, lanes] = jnp.concatenate([a[:, 64:], b[:, 64:]], 1)
    top[...] = jnp.full_like(top, -jnp.inf)
    total[...] = jnp.zeros_like(total)
    picked[...] = jnp.zeros_like(picked)

    for k in range(2):

        def step(i, carry):
            later = i + AHEAD

            @pl.when(later < steps)
            def _():
                bringing(k, later).start()

            if k == 0:

                @pl.when(later >= steps)
                def _():
                    bringing(1, later - steps).start()

            bringing(k, i).wait()
            logits = jnp.dot(near[k, block(i), :], rows[...], preferred_element_type=jnp.float32)
            tiles = logits.reshape(BLOCK_ROWS // 8, 8, width)
            before = top[...]
            now = jnp.maximum(before, jnp.max(tiles, 0))
            total[...] = total[...] * jnp.exp(before - now) + jnp.sum(jnp.exp(tiles - now[None]), 0)
            top[...] = now
            ids = lax.broadcasted_iota(jnp.int32, (BLOCK_ROWS, width), 0)
            hit = ids == local_ids[k : k + 1, :] - i * BLOCK_ROWS
            picked[...] += jnp.sum(jnp.where(hit, logits, 0.0).reshape(BLOCK_ROWS // 8, 8, width), 0)
            return carry

        lax.fori_loop(0, steps, step, 0)
    peak = jnp.max(top[...], 0, keepdims=True)
    mass = jnp.sum(total[...] * jnp.exp(top[...] - peak), 0, keepdims=True)
    out[0:1, :] = peak + jnp.log(mass)
    out[1:2, :] = jnp.sum(picked[...], 0, keepdims=True)


def chunk_stats(weights, local_ids, *parts):
    counts = tuple(part.shape[0] // ROWS for part in parts)
    width = 64 * sum(counts)
    vocab, depth = weights[0].shape
    near = pl.BlockSpec(memory_space=pltpu.VMEM)
    held = lambda arrays: [pltpu.with_memory_space_constraint(array, pltpu.VMEM) for array in arrays]
    far = pl.BlockSpec(memory_space=pl.ANY)
    return pl.pallas_call(
        functools.partial(stats_kernel, counts=counts),
        in_specs=[near] * (1 + len(parts)) + [far, far],
        out_specs=near,
        out_shape=jax.ShapeDtypeStruct((2, width), jnp.float32),
        scratch_shapes=[pltpu.VMEM((2, vocab, depth), jnp.bfloat16), pltpu.VMEM((depth, width), jnp.bfloat16)]
        + [pltpu.VMEM((8, width), jnp.float32)] * 3
        + [pltpu.SemaphoreType.DMA((2, vocab // BLOCK_ROWS))],
        compiler_params=pltpu.CompilerParams(vmem_limit_bytes=(width // 256 * 8 + 31) * 2**20),
        cost_estimate=pl.CostEstimate(
            flops=4 * width * vocab * depth, bytes_accessed=4 * vocab * depth, transcendentals=2 * vocab * width
        ),
    )(local_ids, *held(parts), *[pltpu.with_memory_space_constraint(w, pltpu.HBM) for w in weights])


def body(hidden, weight, targets, slot, prompt_len, ref_means):
    y, z, x, c = (lax.axis_index(axis) for axis in EVERY)
    vocab_cols = weight.shape[1]
    w_own = weight.T
    mine = hidden.T

    theirs = lax.ppermute(mine, C, SWAP)
    theirs, weight_sent = lax.optimization_barrier((theirs, w_own))
    w_other = lax.ppermute(weight_sent, C, SWAP)
    weights = [w_own, w_other]
    low = jnp.concatenate([mine[:, :64], theirs[:, :64]], 1)
    high = jnp.concatenate([theirs[:, 64:], mine[:, 64:]], 1)
    half = jnp.where(c == 0, low, high)
    behind, ahead, across = (lax.ppermute(half, X, ring_pairs(s)) for s in (1, 3, 2))
    turned = jnp.concatenate([half, ahead, across, behind, half, ahead, across], 0)
    own = lax.dynamic_slice_in_dim(turned, lax.rem(4 - x, 4) * 448, 1792, 0)

    off_y, off_z = jnp.where(c == 0, ALONG_B, ALONG_A), jnp.where(c == 0, ALONG_A, ALONG_B)
    source = (y + off_y) % 4 * 4 + (z + off_z) % 4
    ids = jnp.take(targets.reshape(32, 64), source * 2 + c, axis=0).reshape(1, 1024)
    start = lambda core: (((x * 2 + core) * 4 + y) * 4 + z) * vocab_cols
    local_ids = jnp.concatenate([ids - start(c), ids - start(1 - c)], 0)

    a_behind, a_ahead, *a_across = (shifted(own, True, k) for k in (1, 3, 2))
    upper = jnp.concatenate([own, a_behind], 0)
    lower = jnp.concatenate([a_ahead, *a_across], 0)
    behind_upper, ahead_lower = shifted(upper, False, 1), shifted(lower, False, 3)
    behind_lower, ahead_upper = shifted(lower, False, 1), shifted(upper, False, 3)
    first = chunk_stats(weights, local_ids[:, :256], upper, lower)
    behind_upper, ahead_lower, first = lax.optimization_barrier((behind_upper, ahead_lower, first))
    across = [shifted(behind_upper, False, 1), shifted(ahead_lower, False, 3)]
    second = chunk_stats(weights, local_ids[:, 256:512], behind_upper, ahead_lower)
    behind_lower, ahead_upper, across, second = lax.optimization_barrier((behind_lower, ahead_upper, across, second))
    third = chunk_stats(weights, local_ids[:, 512:], behind_lower, ahead_upper, *across)
    stats = jnp.concatenate([first, second, third], 1).reshape(2, 16, 64)
    group = np.arange(16, dtype=np.int32)
    ahead_y, ahead_z = (group // 4 - y) % 4, (group % 4 - z) % 4
    at = jnp.take(PLACE, jnp.where(c == 0, ahead_z * 4 + ahead_y, ahead_y * 4 + ahead_z), axis=0)
    stats = jnp.take(stats, at, axis=1).reshape(2, 1024)

    copies = jnp.broadcast_to(stats, (64, 2, 1024))
    parts = lax.all_to_all(copies, CHIPS, split_axis=0, concat_axis=0, tiled=True)
    peak = jnp.max(parts[:, 0], 0)
    mass = jnp.sum(jnp.exp(parts[:, 0] - peak), 0)
    token_lp = (jnp.sum(parts[:, 1], 0) - (peak + jnp.log(mass))).reshape(16, 64)
    other_lp = lax.ppermute(token_lp, C, SWAP)
    per_seq = jnp.where(
        c == 0, jnp.concatenate([token_lp, other_lp], 1), jnp.concatenate([other_lp, token_lp], 1)
    )
    own_rows = lax.dynamic_slice_in_dim(per_seq, y * 4 + z, 1, 0).reshape(128)
    margins, pair_loss = finish(per_seq, slot, prompt_len, ref_means)
    return (own_rows, margins, pair_loss)


def solution(mesh):
    split = Mesh(mesh.devices.reshape(4, 4, 4, 2), EVERY)
    in_specs = (P(TOK, VOC), P(None, VOC_TOK), P(), P(), P(), P())
    out_specs = (P(TOK), P(), P())
    return jax.shard_map(body, mesh=split, in_specs=in_specs, out_specs=out_specs, check_vma=False)
```

time: 134 us -> 121 us (0.903)
  waiting for transfers between devices: 31.9 us -> 20.2 us
  local copies, waits for them, and re-layouts: 9.15 us -> 5.25 us
  Pallas kernels: 50 us -> 47.4 us
  blocking collectives: 15.9 us -> 18.2 us
  starting transfers between devices: 20.2 us -> 22.4 us
    ppermute x8 -> x9, waiting for transfers between devices: 19.6 us -> 10.2 us  [shifted(): return lax.ppermute(block, EVERY, crossed_pairs(first, step))]
    ppermute x1, waiting for transfers between devices: 4.75 us -> 1.52 us  [body(): theirs = lax.ppermute(mine, C, SWAP)]
    ppermute x8 -> x9, starting transfers between devices: 14.3 us -> 17.4 us  [shifted(): return lax.ppermute(block, EVERY, crossed_pairs(first, step))]
    pallas_call x3, Pallas kernels: 50 us -> 47.4 us  [chunk_stats(): pl.pallas_call(functools.partial(stats_kernel, counts=counts), in_specs=[...]
    slice x4 -> x0, local copies, waits for them, and re-layouts: 2.51 us -> none  [the longest x1 1.24 us: body(): b_behind[:3584]]
    all_to_all x1, blocking collectives: 15.9 us -> 18.2 us  [body(): lax.all_to_all(copies, CHIPS, split_axis=0, concat_axis=0, tiled=True)]
    gather x7 -> x4, local copies, waits for them, and re-layouts: 3.31 us -> 1.33 us  [the longest x3 0.67 us: body(): stats = jnp.take(stats, at, axis=1).reshape(2, 1024)]
  transfers between devices with their start and end apart: 14 -> 15, of which waited for: 9 -> 7; matrix products, arithmetic and copies ran while one was open for 4% -> 4% of each run, Pallas kernels for 27% -> 21%
where the time goes in v2:
time: 121 us; the launch traced here: 119 us
  Pallas kernels  47.4 us (39%)
  starting transfers between devices  22.4 us (19%)
  waiting for transfers between devices  20.2 us (17%)
  blocking collectives  18.2 us (15%)
  local copies, waits for them, and re-layouts  5.25 us (4%)
  other arithmetic  3.05 us (3%)
  between operations  2.74 us (2%)
    pallas_call x3, Pallas kernels, chunk_stats(): pl.pallas_call(functools.partial(stats_kernel, counts=counts), in_specs=[...  47.4 us
    all_to_all x1, blocking collectives, body(): lax.all_to_all(copies, CHIPS, split_axis=0, concat_axis=0, tiled=True)  18.2 us
    ppermute x9, starting transfers between devices, shifted(): return lax.ppermute(block, EVERY, crossed_pairs(first, step))  17.4 us
    ppermute x9, waiting for transfers between devices, shifted(): return lax.ppermute(block, EVERY, crossed_pairs(first, step))  10.2 us
    ppermute x3, waiting for transfers between devices, body(): lax.ppermute(half, X, ring_pairs(s))  7.35 us
    ppermute x3, starting transfers between devices, body(): lax.ppermute(half, X, ring_pairs(s))  4.69 us
  transfers between devices with their start and end apart: 15, of which 7 were waited for; matrix products, arithmetic and copies ran while one was open for 4% of the time, Pallas kernels for 21%

profile of v2, /device:TPU:0, one launch (start us, length us, event | category | flops | bytes accessed | tf_op | source)
XLA Modules:
  0.0 119.2 jit_solution(6376890863838139224)
XLA Ops:
  0.7 1.5 %collective-permute-done = bf16[448,128]{1,0:T(8,128)(2,1)S(1)} collective-permute-done((bf16[448,128]{1,0:T(8,128)(2,1)}, bf16[448,128]{1,0:T(8,128)(2,1)S(1)}, u32[]{:S(2)}, u32[]{:S(2)}) %collective-permute-start) | collective-permute-done | bytes 114720 | tf_op jit(solution)/shard_map/ppermute | solution.py:159
  2.3 0.2 collective-permute-start.9
  2.4 1.1 fusion.14
  3.8 2.9 %collective-permute-start.1 = (bf16[448,128]{1,0:T(8,128)(2,1)S(1)}, bf16[448,128]{1,0:T(8,128)(2,1)S(1)}, u32[]{:S(2)}, u32[]{:S(2)}) collective-permute-start(bf16[448,128]{1,0:T(8,128)(2,1)S(1)} %get-tuple-element.32), channel_id=1, source_target_pairs={{0,6},{2,0},{4,2},{6,4},{1,7},{3,1},{5,3},{7,5},{8,14},{10,8},{12,... | collective-permute-start | bytes 344072 | tf_op jit(solution)/shard_map/ppermute | solution.py:166
  6.7 0.7 compare_select_fusion.3
  7.4 0.8 reshape.112
  8.2 0.7 gather_fusion
  8.8 0.9 collective-permute-start.2
  9.7 0.9 collective-permute-start.3
  10.6 5.8 %collective-permute-done.2 = bf16[448,128]{1,0:T(8,128)(2,1)S(1)} collective-permute-done((bf16[448,128]{1,0:T(8,128)(2,1)S(1)}, bf16[448,128]{1,0:T(8,128)(2,1)S(1)}, u32[]{:S(2)}, u32[]{:S(2)}) %collective-permute-start.2) | collective-permute-done | bytes 114720 | tf_op jit(solution)/shard_map/ppermute | solution.py:166
  16.4 1.5 %collective-permute-done.3 = bf16[448,128]{1,0:T(8,128)(2,1)S(1)} collective-permute-done((bf16[448,128]{1,0:T(8,128)(2,1)S(1)}, bf16[448,128]{1,0:T(8,128)(2,1)S(1)}, u32[]{:S(2)}, u32[]{:S(2)}) %collective-permute-start.3) | collective-permute-done | bytes 114720 | tf_op jit(solution)/shard_map/ppermute | solution.py:166
  18.1 2.0 %collective-permute-start.4 = (bf16[1792,128]{1,0:T(8,128)(2,1)S(1)}, bf16[1792,128]{1,0:T(8,128)(2,1)S(1)}, u32[]{:S(2)}, u32[]{:S(2)}) collective-permute-start(bf16[1792,128]{1,0:T(8,128)(2,1)S(1)} %constant_dynamic-slice_fusion), channel_id=1, source_target_pairs={{0,8},{1,33},{2,10},{3,35},{4,12},{5,37},{6,14},{7,39},{8,16},{9,4... | collective-permute-start | bytes 1376264 | tf_op jit(solution)/shard_map/ppermute | solution.py:49
  20.2 0.6 gather_fusion.1
  20.7 2.2 %collective-permute-start.6 = (bf16[1792,128]{1,0:T(8,128)(2,1)S(1)}, bf16[1792,128]{1,0:T(8,128)(2,1)S(1)}, u32[]{:S(2)}, u32[]{:S(2)}) collective-permute-start(bf16[1792,128]{1,0:T(8,128)(2,1)S(1)} %constant_dynamic-slice_fusion), channel_id=1, source_target_pairs={{0,24},{1,97},{2,26},{3,99},{4,28},{5,101},{6,30},{7,103},{8,0},{9... | collective-permute-start | bytes 1376264 | tf_op jit(solution)/shard_map/ppermute | solution.py:49
  22.9 1.8 %collective-permute-start.7 = (bf16[1792,128]{1,0:T(8,128)(2,1)S(1)}, bf16[1792,128]{1,0:T(8,128)(2,1)S(1)}, u32[]{:S(2)}, u32[]{:S(2)}) collective-permute-start(bf16[1792,128]{1,0:T(8,128)(2,1)S(1)} %constant_dynamic-slice_fusion), channel_id=1, source_target_pairs={{0,16},{1,65},{2,18},{3,67},{4,20},{5,69},{6,22},{7,71},{8,24},{9,... | collective-permute-start | bytes 1376264 | tf_op jit(solution)/shard_map/ppermute | solution.py:49
  24.8 3.9 %collective-permute-done.4 = bf16[1792,128]{1,0:T(8,128)(2,1)S(1)} collective-permute-done((bf16[1792,128]{1,0:T(8,128)(2,1)S(1)}, bf16[1792,128]{1,0:T(8,128)(2,1)S(1)}, u32[]{:S(2)}, u32[]{:S(2)}) %collective-permute-start.4) | collective-permute-done | bytes 458784 | tf_op jit(solution)/shard_map/ppermute | solution.py:49
  28.7 1.6 %collective-permute-start.5 = (bf16[3584,128]{1,0:T(8,128)(2,1)S(1)}, bf16[3584,128]{1,0:T(8,128)(2,1)S(1)}, u32[]{:S(2)}, u32[]{:S(2)}) collective-permute-start(bf16[3584,128]{1,0:T(8,128)(2,1)S(1)} %pad_maximum_fusion.refs_0_), channel_id=1, source_target_pairs={{0,32},{1,9},{2,34},{3,11},{4,36},{5,13},{6,38},{7,15},{8,40},{9,1... | collective-permute-start | bytes 2752520 | tf_op jit(solution)/shard_map/ppermute | solution.py:49
  30.4 3.5 %collective-permute-done.6 = bf16[1792,128]{1,0:T(8,128)(2,1)S(1)} collective-permute-done((bf16[1792,128]{1,0:T(8,128)(2,1)S(1)}, bf16[1792,128]{1,0:T(8,128)(2,1)S(1)}, u32[]{:S(2)}, u32[]{:S(2)}) %collective-permute-start.6) | collective-permute-done | bytes 458784 | tf_op jit(solution)/shard_map/ppermute | solution.py:49
  33.9 2.8 %collective-permute-done.7 = bf16[1792,128]{1,0:T(8,128)(2,1)S(1)} collective-permute-done((bf16[1792,128]{1,0:T(8,128)(2,1)S(1)}, bf16[1792,128]{1,0:T(8,128)(2,1)S(1)}, u32[]{:S(2)}, u32[]{:S(2)}) %collective-permute-start.7) | collective-permute-done | bytes 458784 | tf_op jit(solution)/shard_map/ppermute | solution.py:49
  36.8 4.4 %collective-permute-start.8 = (bf16[3584,128]{1,0:T(8,128)(2,1)S(1)}, bf16[3584,128]{1,0:T(8,128)(2,1)}, u32[]{:S(2)}, u32[]{:S(2)}) collective-permute-start(bf16[3584,128]{1,0:T(8,128)(2,1)S(1)} %constant_dynamic-update-slice_fusion.7.refs_1_), channel_id=1, source_target_pairs={{0,96},{1,25},{2,98},{3,27},{4,100},{5,29},{6,102},{7,31},{8,104},... | collective-permute-start | bytes 2752520 | tf_op jit(solution)/shard_map/ppermute | solution.py:49
  41.5 2.0 %collective-permute-start.10 = (bf16[3584,128]{1,0:T(8,128)(2,1)S(1)}, bf16[3584,128]{1,0:T(8,128)(2,1)}, u32[]{:S(2)}, u32[]{:S(2)}) collective-permute-start(bf16[3584,128]{1,0:T(8,128)(2,1)S(1)} %constant_dynamic-update-slice_fusion.7.refs_1_), channel_id=1, source_target_pairs={{0,32},{1,9},{2,34},{3,11},{4,36},{5,13},{6,38},{7,15},{8,40},{9,1... | collective-permute-start | bytes 2752520 | tf_op jit(solution)/shard_map/ppermute | solution.py:49
  43.5 11.9 %shard_map.130 = f32[2,256]{1,0:T(2,128)S(1)} custom-call(s32[2,256]{1,0:T(2,128)S(1)} %get-tuple-element.43.local_ids, bf16[3584,128]{1,0:T(8,128)(2,1)S(1)} %pad_maximum_fusion.refs_0_, bf16[3584,128]{1,0:T(8,128)(2,1)S(1)} %constant_dynamic-update-slice_fusion.7.refs_1_, bf16[2000,3584]{1,0:T(8,128)(2,1)} %bitcast.12, ...), custom_call_target="tpu_custom_call" | custom-call | flops 7340032000 | bytes 28672000 | tf_op jit(solution)/shard_map/pallas_call | solution.py:138
  55.5 3.2 %collective-permute-start.13 = (bf16[3584,128]{1,0:T(8,128)(2,1)}, bf16[3584,128]{1,0:T(8,128)(2,1)}, u32[]{:S(2)}, u32[]{:S(2)}) collective-permute-start(bf16[3584,128]{1,0:T(8,128)(2,1)} %collective-permute-done.8.refs_1_), channel_id=1, source_target_pairs={{0,96},{1,25},{2,98},{3,27},{4,100},{5,29},{6,102},{7,31},{8,104},... | collective-permute-start | bytes 2752520 | tf_op jit(solution)/shard_map/ppermute | solution.py:49
  58.9 13.4 %shard_map.131 = f32[2,256]{1,0:T(2,128)S(1)} custom-call(s32[2,256]{1,0:T(2,128)S(1)} %get-tuple-element.42.local_ids, bf16[3584,128]{1,0:T(8,128)(2,1)S(1)} %collective-permute-done.5.refs_0_, bf16[3584,128]{1,0:T(8,128)(2,1)} %collective-permute-done.8.refs_1_, bf16[2000,3584]{1,0:T(8,128)(2,1)} %bitcast.13, ...), custom_call_target="tpu_custom_call" | custom-call | flops 7340032000 | bytes 28672000 | tf_op jit(solution)/shard_map/pallas_call | solution.py:138
  72.3 22.1 %shard_map.132 = f32[2,512]{1,0:T(2,128)S(1)} custom-call(s32[2,512]{1,0:T(2,128)S(1)} %pad_add_fusion.local_ids, bf16[3584,128]{1,0:T(8,128)(2,1)} %collective-permute-done.10.refs_0_, bf16[3584,128]{1,0:T(8,128)(2,1)} %collective-permute-done.11.refs_1_, bf16[3584,128]{1,0:T(8,128)(2,1)} %collective-permute-done.12.refs_2_, ...), custom_call_target="tpu_custom_call" | custom-call | flops 14680064000 | bytes 28672000 | tf_op jit(solution)/shard_map/pallas_call | solution.py:138
  94.6 0.6 gather_fusion.2
  95.4 18.2 %all_to_all.5 = f32[64,2,1024]{2,1,0:T(2,128)S(1)} all-to-all(f32[64,2,1024]{2,1,0:T(2,128)S(1)} %broadcast_in_dim.71), channel_id=1, replica_groups=mesh['tok_0'=4,'tok_1'=4,'voc_0'=4,'voc_1'=2] {'tok_0','tok_1','voc_0'}, dimensions={0} | all-to-all | bytes 1048576 | tf_op jit(solution)/shard_map/all_to_all | solution.py:194
  113.6 0.5 slice_reduce_fusion.1
  114.4 1.1 collective-permute-done.14
  115.5 0.2 select_reduce_fusion
  115.8 1.1 fusion.13
  117.6 0.5 dynamic-slice_bitcast_fusion
  (60 shorter events, 2.0 us)
Async XLA Ops:
  0.6 7.5 %copy-start = (s32[16]{0:T(128)S(1)}, s32[16]{0:T(128)}, u32[]{:S(2)}) copy-start(s32[16]{0:T(128)} %constant.154.clone) | copy-start | bytes 196
  0.6 1.6 %collective-permute-start = (bf16[448,128]{1,0:T(8,128)(2,1)}, bf16[448,128]{1,0:T(8,128)(2,1)S(1)}, u32[]{:S(2)}, u32[]{:S(2)}) collective-permute-start(bf16[448,128]{1,0:T(8,128)(2,1)} %bitcast.15), channel_id=1, source_target_pairs={{0,1},{1,0},{2,3},{3,2},{4,5},{5,4},{6,7},{7,6},{8,9},{9,8},{10,11... | collective-permute-start | bytes 344072 | tf_op jit(solution)/shard_map/ppermute | solution.py:159
  2.3 41.2 %collective-permute-start.9 = (bf16[2000,3584]{1,0:T(8,128)(2,1)}, bf16[2000,3584]{1,0:T(8,128)(2,1)}, u32[]{:S(2)}, u32[]{:S(2)}) collective-permute-start(bf16[2000,3584]{1,0:T(8,128)(2,1)} %bitcast.11), channel_id=1, source_target_pairs={{0,1},{1,0},{2,3},{3,2},{4,5},{5,4},{6,7},{7,6},{8,9},{9,8},{10,11... | collective-permute-start | bytes 43008008 | tf_op jit(solution)/shard_map/ppermute | solution.py:161
  3.6 16.5 %copy-start.4 = (s32[16]{0:T(128)S(1)}, s32[16]{0:T(128)}, u32[]{:S(2)}) copy-start(s32[16]{0:T(128)} %constant.150.clone) | copy-start | bytes 196
  3.6 16.5 %copy-start.5 = (s32[16]{0:T(128)S(1)}, s32[16]{0:T(128)}, u32[]{:S(2)}) copy-start(s32[16]{0:T(128)} %constant.151.clone) | copy-start | bytes 196
  3.8 6.8 %collective-permute-start.1 = (bf16[448,128]{1,0:T(8,128)(2,1)S(1)}, bf16[448,128]{1,0:T(8,128)(2,1)S(1)}, u32[]{:S(2)}, u32[]{:S(2)}) collective-permute-start(bf16[448,128]{1,0:T(8,128)(2,1)S(1)} %get-tuple-element.32), channel_id=1, source_target_pairs={{0,6},{2,0},{4,2},{6,4},{1,7},{3,1},{5,3},{7,5},{8,14},{10,8},{12,... | collective-permute-start | bytes 344072 | tf_op jit(solution)/shard_map/ppermute | solution.py:166
  8.8 7.6 %collective-permute-start.2 = (bf16[448,128]{1,0:T(8,128)(2,1)S(1)}, bf16[448,128]{1,0:T(8,128)(2,1)S(1)}, u32[]{:S(2)}, u32[]{:S(2)}) collective-permute-start(bf16[448,128]{1,0:T(8,128)(2,1)S(1)} %get-tuple-element.32), channel_id=1, source_target_pairs={{0,4},{2,6},{4,0},{6,2},{1,5},{3,7},{5,1},{7,3},{8,12},{10,14},{12... | collective-permute-start | bytes 344072 | tf_op jit(solution)/shard_map/ppermute | solution.py:166
  9.7 8.3 %collective-permute-start.3 = (bf16[448,128]{1,0:T(8,128)(2,1)S(1)}, bf16[448,128]{1,0:T(8,128)(2,1)S(1)}, u32[]{:S(2)}, u32[]{:S(2)}) collective-permute-start(bf16[448,128]{1,0:T(8,128)(2,1)S(1)} %get-tuple-element.32), channel_id=1, source_target_pairs={{0,2},{2,4},{4,6},{6,0},{1,3},{3,5},{5,7},{7,1},{8,10},{10,12},{12... | collective-permute-start | bytes 344072 | tf_op jit(solution)/shard_map/ppermute | solution.py:166
  18.1 10.6 %collective-permute-start.4 = (bf16[1792,128]{1,0:T(8,128)(2,1)S(1)}, bf16[1792,128]{1,0:T(8,128)(2,1)S(1)}, u32[]{:S(2)}, u32[]{:S(2)}) collective-permute-start(bf16[1792,128]{1,0:T(8,128)(2,1)S(1)} %constant_dynamic-slice_fusion), channel_id=1, source_target_pairs={{0,8},{1,33},{2,10},{3,35},{4,12},{5,37},{6,14},{7,39},{8,16},{9,4... | collective-permute-start | bytes 1376264 | tf_op jit(solution)/shard_map/ppermute | solution.py:49
  20.7 13.2 %collective-permute-start.6 = (bf16[1792,128]{1,0:T(8,128)(2,1)S(1)}, bf16[1792,128]{1,0:T(8,128)(2,1)S(1)}, u32[]{:S(2)}, u32[]{:S(2)}) collective-permute-start(bf16[1792,128]{1,0:T(8,128)(2,1)S(1)} %constant_dynamic-slice_fusion), channel_id=1, source_target_pairs={{0,24},{1,97},{2,26},{3,99},{4,28},{5,101},{6,30},{7,103},{8,0},{9... | collective-permute-start | bytes 1376264 | tf_op jit(solution)/shard_map/ppermute | solution.py:49
  22.9 13.8 %collective-permute-start.7 = (bf16[1792,128]{1,0:T(8,128)(2,1)S(1)}, bf16[1792,128]{1,0:T(8,128)(2,1)S(1)}, u32[]{:S(2)}, u32[]{:S(2)}) collective-permute-start(bf16[1792,128]{1,0:T(8,128)(2,1)S(1)} %constant_dynamic-slice_fusion), channel_id=1, source_target_pairs={{0,16},{1,65},{2,18},{3,67},{4,20},{5,69},{6,22},{7,71},{8,24},{9,... | collective-permute-start | bytes 1376264 | tf_op jit(solution)/shard_map/ppermute | solution.py:49
  28.7 26.7 %collective-permute-start.5 = (bf16[3584,128]{1,0:T(8,128)(2,1)S(1)}, bf16[3584,128]{1,0:T(8,128)(2,1)S(1)}, u32[]{:S(2)}, u32[]{:S(2)}) collective-permute-start(bf16[3584,128]{1,0:T(8,128)(2,1)S(1)} %pad_maximum_fusion.refs_0_), channel_id=1, source_target_pairs={{0,32},{1,9},{2,34},{3,11},{4,36},{5,13},{6,38},{7,15},{8,40},{9,1... | collective-permute-start | bytes 2752520 | tf_op jit(solution)/shard_map/ppermute | solution.py:49
  36.8 18.6 %collective-permute-start.8 = (bf16[3584,128]{1,0:T(8,128)(2,1)S(1)}, bf16[3584,128]{1,0:T(8,128)(2,1)}, u32[]{:S(2)}, u32[]{:S(2)}) collective-permute-start(bf16[3584,128]{1,0:T(8,128)(2,1)S(1)} %constant_dynamic-update-slice_fusion.7.refs_1_), channel_id=1, source_target_pairs={{0,96},{1,25},{2,98},{3,27},{4,100},{5,29},{6,102},{7,31},{8,104},... | collective-permute-start | bytes 2752520 | tf_op jit(solution)/shard_map/ppermute | solution.py:49
  41.4 30.9 %collective-permute-start.11 = (bf16[3584,128]{1,0:T(8,128)(2,1)S(1)}, bf16[3584,128]{1,0:T(8,128)(2,1)}, u32[]{:S(2)}, u32[]{:S(2)}) collective-permute-start(bf16[3584,128]{1,0:T(8,128)(2,1)S(1)} %pad_maximum_fusion.refs_0_), channel_id=1, source_target_pairs={{0,96},{1,25},{2,98},{3,27},{4,100},{5,29},{6,102},{7,31},{8,104},... | collective-permute-start | bytes 2752520 | tf_op jit(solution)/shard_map/ppermute | solution.py:49
  41.5 30.8 %collective-permute-start.10 = (bf16[3584,128]{1,0:T(8,128)(2,1)S(1)}, bf16[3584,128]{1,0:T(8,128)(2,1)}, u32[]{:S(2)}, u32[]{:S(2)}) collective-permute-start(bf16[3584,128]{1,0:T(8,128)(2,1)S(1)} %constant_dynamic-update-slice_fusion.7.refs_1_), channel_id=1, source_target_pairs={{0,32},{1,9},{2,34},{3,11},{4,36},{5,13},{6,38},{7,15},{8,40},{9,1... | collective-permute-start | bytes 2752520 | tf_op jit(solution)/shard_map/ppermute | solution.py:49
  55.4 16.9 %collective-permute-start.12 = (bf16[3584,128]{1,0:T(8,128)(2,1)S(1)}, bf16[3584,128]{1,0:T(8,128)(2,1)}, u32[]{:S(2)}, u32[]{:S(2)}) collective-permute-start(bf16[3584,128]{1,0:T(8,128)(2,1)S(1)} %collective-permute-done.5.refs_0_), channel_id=1, source_target_pairs={{0,32},{1,9},{2,34},{3,11},{4,36},{5,13},{6,38},{7,15},{8,40},{9,1... | collective-permute-start | bytes 2752520 | tf_op jit(solution)/shard_map/ppermute | solution.py:49
  55.5 16.8 %collective-permute-start.13 = (bf16[3584,128]{1,0:T(8,128)(2,1)}, bf16[3584,128]{1,0:T(8,128)(2,1)}, u32[]{:S(2)}, u32[]{:S(2)}) collective-permute-start(bf16[3584,128]{1,0:T(8,128)(2,1)} %collective-permute-done.8.refs_1_), channel_id=1, source_target_pairs={{0,96},{1,25},{2,98},{3,27},{4,100},{5,29},{6,102},{7,31},{8,104},... | collective-permute-start | bytes 2752520 | tf_op jit(solution)/shard_map/ppermute | solution.py:49
  94.4 19.9 %copy-start.3 = (s32[16]{0:T(128)S(1)}, s32[16]{0:T(128)}, u32[]{:S(2)}) copy-start(s32[16]{0:T(128)} %param.14) | copy-start | bytes 196
  94.5 21.0 %copy-start.1 = (s32[16]{0:T(128)S(1)}, s32[16]{0:T(128)}, u32[]{:S(2)}) copy-start(s32[16]{0:T(128)} %param.15) | copy-start | bytes 196
  94.5 21.2 %copy-start.2 = (f32[16]{0:T(128)S(1)}, f32[16]{0:T(128)}, u32[]{:S(2)}) copy-start(f32[16]{0:T(128)} %param.16) | copy-start | bytes 196
  114.3 1.2 %collective-permute-start.14 = (f32[16,64]{1,0:T(8,128)S(1)}, f32[16,64]{1,0:T(8,128)S(1)}, u32[]{:S(2)}, u32[]{:S(2)}) collective-permute-start(f32[16,64]{1,0:T(8,128)S(1)} %sub.92), channel_id=1, source_target_pairs={{0,1},{1,0},{2,3},{3,2},{4,5},{5,4},{6,7},{7,6},{8,9},{9,8},{10,11... | collective-permute-start | bytes 12296 | tf_op jit(solution)/shard_map/ppermute | solution.py:198

commit v3 on v2

--- a/solution.py
+++ b/solution.py
@@ -24,7 +24,7 @@
 PLACE[ALONG_A * 4 + ALONG_B] = np.arange(16)
 ROWS = 1792
 BLOCK_ROWS = 400
-AHEAD = 3
+AHEAD = 2
 
 beta_scale = 2.0
 
@@ -68,7 +68,7 @@
 def stats_kernel(local_ids, *refs, counts):
     n_in = len(counts)
     parts = refs[:n_in]
-    *far, out, near, rows, top, total, picked, arrived = refs[n_in:]
+    *far, out, near, staged, rows, top, total, picked, arrived, landed = refs[n_in:]
     width = rows.shape[1]
     steps = near.shape[1] // BLOCK_ROWS
 
@@ -78,38 +78,41 @@
     def bringing(k, i):
         return pltpu.make_async_copy(far[k].at[block(i), :], near.at[k, block(i), :], arrived.at[k, i])
 
+    begins = [ROWS * sum(counts[:n]) for n in range(n_in)]
+    staging = [
+        pltpu.make_async_copy(part, staged.at[pl.ds(begin, part.shape[0]), :], landed.at[n])
+        for n, (part, begin) in enumerate(zip(parts, begins))
+    ]
+    for copy in staging:
+        copy.start()
     for i in range(AHEAD):
         bringing(0, i).start()
-
-    pieces = [(ref, k * ROWS) for ref, n in zip(parts, counts) for k in range(n)]
-    for p in range(len(pieces) // 2):
-        (ref_a, at_a), (ref_b, at_b) = pieces[2 * p], pieces[2 * p + 1]
+        bringing(1, i).start()
+
+    waited = 0
+    for p in range(sum(counts) // 2):
+        while waited < n_in and begins[waited] < (2 * p + 2) * ROWS:
+            staging[waited].wait()
+            waited += 1
         lanes = slice(p * 128, (p + 1) * 128)
         for x in range(4):
-            a = ref_a[at_a + x * 448 : at_a + (x + 1) * 448, :]
-            b = ref_b[at_b + x * 448 : at_b + (x + 1) * 448, :]
+            at = 2 * p * ROWS + x * 448
+            a, b = staged[at : at + 448, :], staged[at + ROWS : at + ROWS + 448, :]
             rows[2 * x * 448 : (2 * x + 1) * 448, lanes] = jnp.concatenate([a[:, :64], b[:, :64]], 1)
             rows[(2 * x + 1) * 448 : (2 * x + 2) * 448, lanes] = jnp.concatenate([a[:, 64:], b[:, 64:]], 1)
     top[...] = jnp.full_like(top, -jnp.inf)
     total[...] = jnp.zeros_like(total)
     picked[...] = jnp.zeros_like(picked)
 
-    for k in range(2):
-
-        def step(i, carry):
-            later = i + AHEAD
-
-            @pl.when(later < steps)
-            def _():
-                bringing(k, later).start()
-
-            if k == 0:
-
-                @pl.when(later >= steps)
-                def _():
-                    bringing(1, later - steps).start()
-
-            bringing(k, i).wait()
+    def step(i, carry):
+        @pl.when(i + AHEAD < steps)
+        def _():
+            bringing(0, i + AHEAD).start()
+            bringing(1, i + AHEAD).start()
+
+        bringing(0, i).wait()
+        bringing(1, i).wait()
+        for k in range(2):
             logits = jnp.dot(near[k, block(i), :], rows[...], preferred_element_type=jnp.float32)
             tiles = logits.reshape(BLOCK_ROWS // 8, 8, width)
             before = top[...]
@@ -119,9 +122,9 @@
             ids = lax.broadcasted_iota(jnp.int32, (BLOCK_ROWS, width), 0)
             hit = ids == local_ids[k : k + 1, :] - i * BLOCK_ROWS
             picked[...] += jnp.sum(jnp.where(hit, logits, 0.0).reshape(BLOCK_ROWS // 8, 8, width), 0)
-            return carry
-
-        lax.fori_loop(0, steps, step, 0)
+        return carry
+
+    lax.fori_loop(0, steps, step, 0)
     peak = jnp.max(top[...], 0, keepdims=True)
     mass = jnp.sum(total[...] * jnp.exp(top[...] - peak), 0, keepdims=True)
     out[0:1, :] = peak + jnp.log(mass)
@@ -133,21 +136,24 @@
     width = 64 * sum(counts)
     vocab, depth = weights[0].shape
     near = pl.BlockSpec(memory_space=pltpu.VMEM)
-    held = lambda arrays: [pltpu.with_memory_space_constraint(array, pltpu.VMEM) for array in arrays]
     far = pl.BlockSpec(memory_space=pl.ANY)
     return pl.pallas_call(
         functools.partial(stats_kernel, counts=counts),
-        in_specs=[near] * (1 + len(parts)) + [far, far],
+        in_specs=[near] + [far] * (len(parts) + 2),
         out_specs=near,
         out_shape=jax.ShapeDtypeStruct((2, width), jnp.float32),
-        scratch_shapes=[pltpu.VMEM((2, vocab, depth), jnp.bfloat16), pltpu.VMEM((depth, width), jnp.bfloat16)]
+        scratch_shapes=[
+            pltpu.VMEM((2, vocab, depth), jnp.bfloat16),
+            pltpu.VMEM((ROWS * sum(counts), 128), jnp.bfloat16),
+            pltpu.VMEM((depth, width), jnp.bfloat16),
+        ]
         + [pltpu.VMEM((8, width), jnp.float32)] * 3
-        + [pltpu.SemaphoreType.DMA((2, vocab // BLOCK_ROWS))],
-        compiler_params=pltpu.CompilerParams(vmem_limit_bytes=(width // 256 * 8 + 31) * 2**20),
+        + [pltpu.SemaphoreType.DMA((2, vocab // BLOCK_ROWS)), pltpu.SemaphoreType.DMA((len(parts),))],
+        compiler_params=pltpu.CompilerParams(vmem_limit_bytes=(width // 256 * 7 + 32) * 2**20),
         cost_estimate=pl.CostEstimate(
             flops=4 * width * vocab * depth, bytes_accessed=4 * vocab * depth, transcendentals=2 * vocab * width
         ),
-    )(local_ids, *held(parts), *[pltpu.with_memory_space_constraint(w, pltpu.HBM) for w in weights])
+    )(local_ids, *parts, *[pltpu.with_memory_space_constraint(w, pltpu.HBM) for w in weights])
 
 
 def body(hidden, weight, targets, slot, prompt_len, ref_means):
@@ -187,7 +193,8 @@
     stats = jnp.concatenate([first, second, third], 1).reshape(2, 16, 64)
     group = np.arange(16, dtype=np.int32)
     ahead_y, ahead_z = (group // 4 - y) % 4, (group % 4 - z) % 4
-    at = jnp.take(PLACE, jnp.where(c == 0, ahead_z * 4 + ahead_y, ahead_y * 4 + ahead_z), axis=0)
+    ahead = jnp.where(c == 0, ahead_z * 4 + ahead_y, ahead_y * 4 + ahead_z)
+    at = jnp.sum(jnp.where(ahead[:, None] == np.arange(16)[None, :], PLACE[None, :], 0), axis=1)
     stats = jnp.take(stats, at, axis=1).reshape(2, 1024)
 
     copies = jnp.broadcast_to(stats, (64, 2, 1024))

time: 121 us -> 120 us (level)
  transfers between devices with their start and end apart: 15 -> 15, of which waited for: 7 -> 7; matrix products, arithmetic and copies ran while one was open for 4% -> 4% of each run, Pallas kernels for 21% -> 22%
where the time goes in v3:
time: 120 us; the launch traced here: 119 us
  Pallas kernels  47.6 us (40%)
  starting transfers between devices  22.4 us (19%)
  waiting for transfers between devices  20.4 us (17%)
  blocking collectives  18.1 us (15%)
  local copies, waits for them, and re-layouts  4.59 us (4%)
  other arithmetic  3.22 us (3%)
  between operations  2.74 us (2%)
    pallas_call x3, Pallas kernels, chunk_stats(): pl.pallas_call(functools.partial(stats_kernel, counts=counts), in_specs=[...  47.6 us
    all_to_all x1, blocking collectives, body(): lax.all_to_all(copies, CHIPS, split_axis=0, concat_axis=0, tiled=True)  18.1 us
    ppermute x9, starting transfers between devices, shifted(): return lax.ppermute(block, EVERY, crossed_pairs(first, step))  17.4 us
    ppermute x9, waiting for transfers between devices, shifted(): return lax.ppermute(block, EVERY, crossed_pairs(first, step))  10.4 us
    ppermute x3, waiting for transfers between devices, body(): lax.ppermute(half, X, ring_pairs(s))  7.35 us
    ppermute x3, starting transfers between devices, body(): lax.ppermute(half, X, ring_pairs(s))  4.69 us
  transfers between devices with their start and end apart: 15, of which 7 were waited for; matrix products, arithmetic and copies ran while one was open for 4% of the time, Pallas kernels for 22%

profile of v3, /device:TPU:0, one launch (start us, length us, event | category | flops | bytes accessed | tf_op | source)
XLA Modules:
  0.0 119.0 jit_solution(2444831633427264625)
XLA Ops:
  0.7 1.5 %collective-permute-done = bf16[448,128]{1,0:T(8,128)(2,1)S(1)} collective-permute-done((bf16[448,128]{1,0:T(8,128)(2,1)}, bf16[448,128]{1,0:T(8,128)(2,1)S(1)}, u32[]{:S(2)}, u32[]{:S(2)}) %collective-permute-start) | collective-permute-done | bytes 114720 | tf_op jit(solution)/shard_map/ppermute | solution.py:165
  2.2 0.2 collective-permute-start.9
  2.4 1.1 fusion.15
  3.8 2.9 %collective-permute-start.1 = (bf16[448,128]{1,0:T(8,128)(2,1)S(1)}, bf16[448,128]{1,0:T(8,128)(2,1)S(1)}, u32[]{:S(2)}, u32[]{:S(2)}) collective-permute-start(bf16[448,128]{1,0:T(8,128)(2,1)S(1)} %get-tuple-element.30), channel_id=1, source_target_pairs={{0,6},{2,0},{4,2},{6,4},{1,7},{3,1},{5,3},{7,5},{8,14},{10,8},{12,... | collective-permute-start | bytes 344072 | tf_op jit(solution)/shard_map/ppermute | solution.py:172
  6.7 0.7 compare_and_fusion
  7.4 0.8 reshape.117
  8.2 0.6 gather_fusion
  8.7 0.9 collective-permute-start.2
  9.6 0.9 collective-permute-start.3
  10.5 5.8 %collective-permute-done.2 = bf16[448,128]{1,0:T(8,128)(2,1)S(1)} collective-permute-done((bf16[448,128]{1,0:T(8,128)(2,1)S(1)}, bf16[448,128]{1,0:T(8,128)(2,1)S(1)}, u32[]{:S(2)}, u32[]{:S(2)}) %collective-permute-start.2) | collective-permute-done | bytes 114720 | tf_op jit(solution)/shard_map/ppermute | solution.py:172
  16.3 1.5 %collective-permute-done.3 = bf16[448,128]{1,0:T(8,128)(2,1)S(1)} collective-permute-done((bf16[448,128]{1,0:T(8,128)(2,1)S(1)}, bf16[448,128]{1,0:T(8,128)(2,1)S(1)}, u32[]{:S(2)}, u32[]{:S(2)}) %collective-permute-start.3) | collective-permute-done | bytes 114720 | tf_op jit(solution)/shard_map/ppermute | solution.py:172
  18.0 2.0 %collective-permute-start.4 = (bf16[1792,128]{1,0:T(8,128)(2,1)S(1)}, bf16[1792,128]{1,0:T(8,128)(2,1)S(1)}, u32[]{:S(2)}, u32[]{:S(2)}) collective-permute-start(bf16[1792,128]{1,0:T(8,128)(2,1)S(1)} %constant_dynamic-slice_fusion), channel_id=1, source_target_pairs={{0,8},{1,33},{2,10},{3,35},{4,12},{5,37},{6,14},{7,39},{8,16},{9,4... | collective-permute-start | bytes 1376264 | tf_op jit(solution)/shard_map/ppermute | solution.py:49
  20.3 0.2 select_reduce_fusion.1
  20.5 2.2 %collective-permute-start.6 = (bf16[1792,128]{1,0:T(8,128)(2,1)S(1)}, bf16[1792,128]{1,0:T(8,128)(2,1)S(1)}, u32[]{:S(2)}, u32[]{:S(2)}) collective-permute-start(bf16[1792,128]{1,0:T(8,128)(2,1)S(1)} %constant_dynamic-slice_fusion), channel_id=1, source_target_pairs={{0,24},{1,97},{2,26},{3,99},{4,28},{5,101},{6,30},{7,103},{8,0},{9... | collective-permute-start | bytes 1376264 | tf_op jit(solution)/shard_map/ppermute | solution.py:49
  22.7 1.8 %collective-permute-start.7 = (bf16[1792,128]{1,0:T(8,128)(2,1)S(1)}, bf16[1792,128]{1,0:T(8,128)(2,1)S(1)}, u32[]{:S(2)}, u32[]{:S(2)}) collective-permute-start(bf16[1792,128]{1,0:T(8,128)(2,1)S(1)} %constant_dynamic-slice_fusion), channel_id=1, source_target_pairs={{0,16},{1,65},{2,18},{3,67},{4,20},{5,69},{6,22},{7,71},{8,24},{9,... | collective-permute-start | bytes 1376264 | tf_op jit(solution)/shard_map/ppermute | solution.py:49
  24.5 4.1 %collective-permute-done.4 = bf16[1792,128]{1,0:T(8,128)(2,1)S(1)} collective-permute-done((bf16[1792,128]{1,0:T(8,128)(2,1)S(1)}, bf16[1792,128]{1,0:T(8,128)(2,1)S(1)}, u32[]{:S(2)}, u32[]{:S(2)}) %collective-permute-start.4) | collective-permute-done | bytes 458784 | tf_op jit(solution)/shard_map/ppermute | solution.py:49
  28.7 1.6 %collective-permute-start.5 = (bf16[3584,128]{1,0:T(8,128)(2,1)S(1)}, bf16[3584,128]{1,0:T(8,128)(2,1)S(1)}, u32[]{:S(2)}, u32[]{:S(2)}) collective-permute-start(bf16[3584,128]{1,0:T(8,128)(2,1)S(1)} %pad_maximum_fusion.refs_0_), channel_id=1, source_target_pairs={{0,32},{1,9},{2,34},{3,11},{4,36},{5,13},{6,38},{7,15},{8,40},{9,1... | collective-permute-start | bytes 2752520 | tf_op jit(solution)/shard_map/ppermute | solution.py:49
  30.3 3.3 %collective-permute-done.6 = bf16[1792,128]{1,0:T(8,128)(2,1)S(1)} collective-permute-done((bf16[1792,128]{1,0:T(8,128)(2,1)S(1)}, bf16[1792,128]{1,0:T(8,128)(2,1)S(1)}, u32[]{:S(2)}, u32[]{:S(2)}) %collective-permute-start.6) | collective-permute-done | bytes 458784 | tf_op jit(solution)/shard_map/ppermute | solution.py:49
  33.6 3.0 %collective-permute-done.7 = bf16[1792,128]{1,0:T(8,128)(2,1)S(1)} collective-permute-done((bf16[1792,128]{1,0:T(8,128)(2,1)S(1)}, bf16[1792,128]{1,0:T(8,128)(2,1)S(1)}, u32[]{:S(2)}, u32[]{:S(2)}) %collective-permute-start.7) | collective-permute-done | bytes 458784 | tf_op jit(solution)/shard_map/ppermute | solution.py:49
  36.7 4.4 %collective-permute-start.8 = (bf16[3584,128]{1,0:T(8,128)(2,1)S(1)}, bf16[3584,128]{1,0:T(8,128)(2,1)}, u32[]{:S(2)}, u32[]{:S(2)}) collective-permute-start(bf16[3584,128]{1,0:T(8,128)(2,1)S(1)} %constant_dynamic-update-slice_fusion.7.refs_1_), channel_id=1, source_target_pairs={{0,96},{1,25},{2,98},{3,27},{4,100},{5,29},{6,102},{7,31},{8,104},... | collective-permute-start | bytes 2752520 | tf_op jit(solution)/shard_map/ppermute | solution.py:49
  41.2 2.0 %collective-permute-start.10 = (bf16[3584,128]{1,0:T(8,128)(2,1)S(1)}, bf16[3584,128]{1,0:T(8,128)(2,1)}, u32[]{:S(2)}, u32[]{:S(2)}) collective-permute-start(bf16[3584,128]{1,0:T(8,128)(2,1)S(1)} %constant_dynamic-update-slice_fusion.7.refs_1_), channel_id=1, source_target_pairs={{0,32},{1,9},{2,34},{3,11},{4,36},{5,13},{6,38},{7,15},{8,40},{9,1... | collective-permute-start | bytes 2752520 | tf_op jit(solution)/shard_map/ppermute | solution.py:49
  43.2 12.3 %shard_map.139 = f32[2,256]{1,0:T(2,128)S(1)} custom-call(s32[2,256]{1,0:T(2,128)S(1)} %get-tuple-element.41.local_ids, bf16[3584,128]{1,0:T(8,128)(2,1)S(1)} %pad_maximum_fusion.refs_0_, bf16[3584,128]{1,0:T(8,128)(2,1)S(1)} %constant_dynamic-update-slice_fusion.7.refs_1_, bf16[2000,3584]{1,0:T(8,128)(2,1)} %bitcast.16, ...), custom_call_target="tpu_custom_call" | custom-call | flops 7340032000 | bytes 28672000 | tf_op jit(solution)/shard_map/pallas_call | solution.py:140
  55.6 3.2 %collective-permute-start.13 = (bf16[3584,128]{1,0:T(8,128)(2,1)}, bf16[3584,128]{1,0:T(8,128)(2,1)}, u32[]{:S(2)}, u32[]{:S(2)}) collective-permute-start(bf16[3584,128]{1,0:T(8,128)(2,1)} %collective-permute-done.8.refs_1_), channel_id=1, source_target_pairs={{0,96},{1,25},{2,98},{3,27},{4,100},{5,29},{6,102},{7,31},{8,104},... | collective-permute-start | bytes 2752520 | tf_op jit(solution)/shard_map/ppermute | solution.py:49
  59.0 13.4 %shard_map.140 = f32[2,256]{1,0:T(2,128)S(1)} custom-call(s32[2,256]{1,0:T(2,128)S(1)} %get-tuple-element.40.local_ids, bf16[3584,128]{1,0:T(8,128)(2,1)S(1)} %collective-permute-done.5.refs_0_, bf16[3584,128]{1,0:T(8,128)(2,1)} %collective-permute-done.8.refs_1_, bf16[2000,3584]{1,0:T(8,128)(2,1)} %bitcast.17, ...), custom_call_target="tpu_custom_call" | custom-call | flops 7340032000 | bytes 28672000 | tf_op jit(solution)/shard_map/pallas_call | solution.py:140
  72.4 21.9 %shard_map.141 = f32[2,512]{1,0:T(2,128)S(1)} custom-call(s32[2,512]{1,0:T(2,128)S(1)} %pad_add_fusion.local_ids, bf16[3584,128]{1,0:T(8,128)(2,1)} %collective-permute-done.10.refs_0_, bf16[3584,128]{1,0:T(8,128)(2,1)} %collective-permute-done.11.refs_1_, bf16[3584,128]{1,0:T(8,128)(2,1)} %collective-permute-done.12.refs_2_, ...), custom_call_target="tpu_custom_call" | custom-call | flops 14680064000 | bytes 28672000 | tf_op jit(solution)/shard_map/pallas_call | solution.py:140
  94.5 0.6 gather_fusion.1
  95.3 18.1 %all_to_all.5 = f32[64,2,1024]{2,1,0:T(2,128)S(1)} all-to-all(f32[64,2,1024]{2,1,0:T(2,128)S(1)} %broadcast_in_dim.84), channel_id=1, replica_groups=mesh['tok_0'=4,'tok_1'=4,'voc_0'=4,'voc_1'=2] {'tok_0','tok_1','voc_0'}, dimensions={0} | all-to-all | bytes 1048576 | tf_op jit(solution)/shard_map/all_to_all | solution.py:201
  113.4 0.5 slice_reduce_fusion.1
  114.1 1.1 collective-permute-done.14
  115.2 0.2 select_reduce_fusion
  115.6 1.1 fusion.14
  117.3 0.5 dynamic-slice_bitcast_fusion
  (61 shorter events, 1.9 us)
Async XLA Ops:
  0.6 1.6 %collective-permute-start = (bf16[448,128]{1,0:T(8,128)(2,1)}, bf16[448,128]{1,0:T(8,128)(2,1)S(1)}, u32[]{:S(2)}, u32[]{:S(2)}) collective-permute-start(bf16[448,128]{1,0:T(8,128)(2,1)} %bitcast.19), channel_id=1, source_target_pairs={{0,1},{1,0},{2,3},{3,2},{4,5},{5,4},{6,7},{7,6},{8,9},{9,8},{10,11... | collective-permute-start | bytes 344072 | tf_op jit(solution)/shard_map/ppermute | solution.py:165
  2.2 40.9 %collective-permute-start.9 = (bf16[2000,3584]{1,0:T(8,128)(2,1)}, bf16[2000,3584]{1,0:T(8,128)(2,1)}, u32[]{:S(2)}, u32[]{:S(2)}) collective-permute-start(bf16[2000,3584]{1,0:T(8,128)(2,1)} %bitcast.15), channel_id=1, source_target_pairs={{0,1},{1,0},{2,3},{3,2},{4,5},{5,4},{6,7},{7,6},{8,9},{9,8},{10,11... | collective-permute-start | bytes 43008008 | tf_op jit(solution)/shard_map/ppermute | solution.py:167
  3.5 16.8 %copy-start.3 = (s32[16]{0:T(128)S(1)}, s32[16]{0:T(128)}, u32[]{:S(2)}) copy-start(s32[16]{0:T(128)} %constant.142.clone) | copy-start | bytes 196
  3.5 16.8 %copy-start.4 = (s32[16]{0:T(128)S(1)}, s32[16]{0:T(128)}, u32[]{:S(2)}) copy-start(s32[16]{0:T(128)} %constant.143.clone) | copy-start | bytes 196
  3.5 16.8 %copy-start.5 = (s32[16]{0:T(128)S(1)}, s32[16]{0:T(128)}, u32[]{:S(2)}) copy-start(s32[16]{0:T(128)} %constant.148) | copy-start | bytes 196
  3.8 6.7 %collective-permute-start.1 = (bf16[448,128]{1,0:T(8,128)(2,1)S(1)}, bf16[448,128]{1,0:T(8,128)(2,1)S(1)}, u32[]{:S(2)}, u32[]{:S(2)}) collective-permute-start(bf16[448,128]{1,0:T(8,128)(2,1)S(1)} %get-tuple-element.30), channel_id=1, source_target_pairs={{0,6},{2,0},{4,2},{6,4},{1,7},{3,1},{5,3},{7,5},{8,14},{10,8},{12,... | collective-permute-start | bytes 344072 | tf_op jit(solution)/shard_map/ppermute | solution.py:172
  8.7 7.6 %collective-permute-start.2 = (bf16[448,128]{1,0:T(8,128)(2,1)S(1)}, bf16[448,128]{1,0:T(8,128)(2,1)S(1)}, u32[]{:S(2)}, u32[]{:S(2)}) collective-permute-start(bf16[448,128]{1,0:T(8,128)(2,1)S(1)} %get-tuple-element.30), channel_id=1, source_target_pairs={{0,4},{2,6},{4,0},{6,2},{1,5},{3,7},{5,1},{7,3},{8,12},{10,14},{12... | collective-permute-start | bytes 344072 | tf_op jit(solution)/shard_map/ppermute | solution.py:172
  9.6 8.3 %collective-permute-start.3 = (bf16[448,128]{1,0:T(8,128)(2,1)S(1)}, bf16[448,128]{1,0:T(8,128)(2,1)S(1)}, u32[]{:S(2)}, u32[]{:S(2)}) collective-permute-start(bf16[448,128]{1,0:T(8,128)(2,1)S(1)} %get-tuple-element.30), channel_id=1, source_target_pairs={{0,2},{2,4},{4,6},{6,0},{1,3},{3,5},{5,7},{7,1},{8,10},{10,12},{12... | collective-permute-start | bytes 344072 | tf_op jit(solution)/shard_map/ppermute | solution.py:172
  18.0 10.6 %collective-permute-start.4 = (bf16[1792,128]{1,0:T(8,128)(2,1)S(1)}, bf16[1792,128]{1,0:T(8,128)(2,1)S(1)}, u32[]{:S(2)}, u32[]{:S(2)}) collective-permute-start(bf16[1792,128]{1,0:T(8,128)(2,1)S(1)} %constant_dynamic-slice_fusion), channel_id=1, source_target_pairs={{0,8},{1,33},{2,10},{3,35},{4,12},{5,37},{6,14},{7,39},{8,16},{9,4... | collective-permute-start | bytes 1376264 | tf_op jit(solution)/shard_map/ppermute | solution.py:49
  20.5 13.1 %collective-permute-start.6 = (bf16[1792,128]{1,0:T(8,128)(2,1)S(1)}, bf16[1792,128]{1,0:T(8,128)(2,1)S(1)}, u32[]{:S(2)}, u32[]{:S(2)}) collective-permute-start(bf16[1792,128]{1,0:T(8,128)(2,1)S(1)} %constant_dynamic-slice_fusion), channel_id=1, source_target_pairs={{0,24},{1,97},{2,26},{3,99},{4,28},{5,101},{6,30},{7,103},{8,0},{9... | collective-permute-start | bytes 1376264 | tf_op jit(solution)/shard_map/ppermute | solution.py:49
  22.7 14.0 %collective-permute-start.7 = (bf16[1792,128]{1,0:T(8,128)(2,1)S(1)}, bf16[1792,128]{1,0:T(8,128)(2,1)S(1)}, u32[]{:S(2)}, u32[]{:S(2)}) collective-permute-start(bf16[1792,128]{1,0:T(8,128)(2,1)S(1)} %constant_dynamic-slice_fusion), channel_id=1, source_target_pairs={{0,16},{1,65},{2,18},{3,67},{4,20},{5,69},{6,22},{7,71},{8,24},{9,... | collective-permute-start | bytes 1376264 | tf_op jit(solution)/shard_map/ppermute | solution.py:49
  28.7 26.8 %collective-permute-start.5 = (bf16[3584,128]{1,0:T(8,128)(2,1)S(1)}, bf16[3584,128]{1,0:T(8,128)(2,1)S(1)}, u32[]{:S(2)}, u32[]{:S(2)}) collective-permute-start(bf16[3584,128]{1,0:T(8,128)(2,1)S(1)} %pad_maximum_fusion.refs_0_), channel_id=1, source_target_pairs={{0,32},{1,9},{2,34},{3,11},{4,36},{5,13},{6,38},{7,15},{8,40},{9,1... | collective-permute-start | bytes 2752520 | tf_op jit(solution)/shard_map/ppermute | solution.py:49
  36.7 18.8 %collective-permute-start.8 = (bf16[3584,128]{1,0:T(8,128)(2,1)S(1)}, bf16[3584,128]{1,0:T(8,128)(2,1)}, u32[]{:S(2)}, u32[]{:S(2)}) collective-permute-start(bf16[3584,128]{1,0:T(8,128)(2,1)S(1)} %constant_dynamic-update-slice_fusion.7.refs_1_), channel_id=1, source_target_pairs={{0,96},{1,25},{2,98},{3,27},{4,100},{5,29},{6,102},{7,31},{8,104},... | collective-permute-start | bytes 2752520 | tf_op jit(solution)/shard_map/ppermute | solution.py:49
  41.1 31.3 %collective-permute-start.11 = (bf16[3584,128]{1,0:T(8,128)(2,1)S(1)}, bf16[3584,128]{1,0:T(8,128)(2,1)}, u32[]{:S(2)}, u32[]{:S(2)}) collective-permute-start(bf16[3584,128]{1,0:T(8,128)(2,1)S(1)} %pad_maximum_fusion.refs_0_), channel_id=1, source_target_pairs={{0,96},{1,25},{2,98},{3,27},{4,100},{5,29},{6,102},{7,31},{8,104},... | collective-permute-start | bytes 2752520 | tf_op jit(solution)/shard_map/ppermute | solution.py:49
  41.2 31.2 %collective-permute-start.10 = (bf16[3584,128]{1,0:T(8,128)(2,1)S(1)}, bf16[3584,128]{1,0:T(8,128)(2,1)}, u32[]{:S(2)}, u32[]{:S(2)}) collective-permute-start(bf16[3584,128]{1,0:T(8,128)(2,1)S(1)} %constant_dynamic-update-slice_fusion.7.refs_1_), channel_id=1, source_target_pairs={{0,32},{1,9},{2,34},{3,11},{4,36},{5,13},{6,38},{7,15},{8,40},{9,1... | collective-permute-start | bytes 2752520 | tf_op jit(solution)/shard_map/ppermute | solution.py:49
  55.5 16.9 %collective-permute-start.12 = (bf16[3584,128]{1,0:T(8,128)(2,1)S(1)}, bf16[3584,128]{1,0:T(8,128)(2,1)}, u32[]{:S(2)}, u32[]{:S(2)}) collective-permute-start(bf16[3584,128]{1,0:T(8,128)(2,1)S(1)} %collective-permute-done.5.refs_0_), channel_id=1, source_target_pairs={{0,32},{1,9},{2,34},{3,11},{4,36},{5,13},{6,38},{7,15},{8,40},{9,1... | collective-permute-start | bytes 2752520 | tf_op jit(solution)/shard_map/ppermute | solution.py:49
  55.6 16.8 %collective-permute-start.13 = (bf16[3584,128]{1,0:T(8,128)(2,1)}, bf16[3584,128]{1,0:T(8,128)(2,1)}, u32[]{:S(2)}, u32[]{:S(2)}) collective-permute-start(bf16[3584,128]{1,0:T(8,128)(2,1)} %collective-permute-done.8.refs_1_), channel_id=1, source_target_pairs={{0,96},{1,25},{2,98},{3,27},{4,100},{5,29},{6,102},{7,31},{8,104},... | collective-permute-start | bytes 2752520 | tf_op jit(solution)/shard_map/ppermute | solution.py:49
  94.3 19.7 %copy-start.2 = (s32[16]{0:T(128)S(1)}, s32[16]{0:T(128)}, u32[]{:S(2)}) copy-start(s32[16]{0:T(128)} %param.15) | copy-start | bytes 196
  94.4 20.9 %copy-start = (s32[16]{0:T(128)S(1)}, s32[16]{0:T(128)}, u32[]{:S(2)}) copy-start(s32[16]{0:T(128)} %param.16) | copy-start | bytes 196
  94.4 21.0 %copy-start.1 = (f32[16]{0:T(128)S(1)}, f32[16]{0:T(128)}, u32[]{:S(2)}) copy-start(f32[16]{0:T(128)} %param.17) | copy-start | bytes 196
  114.0 1.2 %collective-permute-start.14 = (f32[16,64]{1,0:T(8,128)S(1)}, f32[16,64]{1,0:T(8,128)S(1)}, u32[]{:S(2)}, u32[]{:S(2)}) collective-permute-start(f32[16,64]{1,0:T(8,128)S(1)} %sub.92), channel_id=1, source_target_pairs={{0,1},{1,0},{2,3},{3,2},{4,5},{5,4},{6,7},{7,6},{8,9},{9,8},{10,11... | collective-permute-start | bytes 12296 | tf_op jit(solution)/shard_map/ppermute | solution.py:205

commit v4 on v3

--- a/solution.py
+++ b/solution.py
@@ -24,7 +24,6 @@
 PLACE[ALONG_A * 4 + ALONG_B] = np.arange(16)
 ROWS = 1792
 BLOCK_ROWS = 400
-AHEAD = 2
 
 beta_scale = 2.0
 
@@ -85,15 +84,15 @@
     ]
     for copy in staging:
         copy.start()
-    for i in range(AHEAD):
-        bringing(0, i).start()
-        bringing(1, i).start()
+    bringing(0, 0).start()
 
     waited = 0
     for p in range(sum(counts) // 2):
         while waited < n_in and begins[waited] < (2 * p + 2) * ROWS:
             staging[waited].wait()
             waited += 1
+        if p == 0:
+            bringing(1, 0).start()
         lanes = slice(p * 128, (p + 1) * 128)
         for x in range(4):
             at = 2 * p * ROWS + x * 448
@@ -105,10 +104,10 @@
     picked[...] = jnp.zeros_like(picked)
 
     def step(i, carry):
-        @pl.when(i + AHEAD < steps)
+        @pl.when(i + 1 < steps)
         def _():
-            bringing(0, i + AHEAD).start()
-            bringing(1, i + AHEAD).start()
+            bringing(0, i + 1).start()
+            bringing(1, i + 1).start()
 
         bringing(0, i).wait()
         bringing(1, i).wait()
@@ -173,13 +172,20 @@
     turned = jnp.concatenate([half, ahead, across, behind, half, ahead, across], 0)
     own = lax.dynamic_slice_in_dim(turned, lax.rem(4 - x, 4) * 448, 1792, 0)
 
+    a_behind, a_ahead, *a_across = (shifted(own, True, k) for k in (1, 3, 2))
+    a_behind, targets, y, z, c = lax.optimization_barrier((a_behind, targets, y, z, c))
+
     off_y, off_z = jnp.where(c == 0, ALONG_B, ALONG_A), jnp.where(c == 0, ALONG_A, ALONG_B)
     source = (y + off_y) % 4 * 4 + (z + off_z) % 4
     ids = jnp.take(targets.reshape(32, 64), source * 2 + c, axis=0).reshape(1, 1024)
     start = lambda core: (((x * 2 + core) * 4 + y) * 4 + z) * vocab_cols
     local_ids = jnp.concatenate([ids - start(c), ids - start(1 - c)], 0)
-
-    a_behind, a_ahead, *a_across = (shifted(own, True, k) for k in (1, 3, 2))
+    group = np.arange(16, dtype=np.int32)
+    ahead_y, ahead_z = (group // 4 - y) % 4, (group % 4 - z) % 4
+    ahead = jnp.where(c == 0, ahead_z * 4 + ahead_y, ahead_y * 4 + ahead_z)
+    at = jnp.sum(jnp.where(ahead[:, None] == np.arange(16)[None, :], PLACE[None, :], 0), axis=1)
+    a_ahead, a_across, local_ids, at = lax.optimization_barrier((a_ahead, a_across, local_ids, at))
+
     upper = jnp.concatenate([own, a_behind], 0)
     lower = jnp.concatenate([a_ahead, *a_across], 0)
     behind_upper, ahead_lower = shifted(upper, False, 1), shifted(lower, False, 3)
@@ -191,10 +197,6 @@
     behind_lower, ahead_upper, across, second = lax.optimization_barrier((behind_lower, ahead_upper, across, second))
     third = chunk_stats(weights, local_ids[:, 512:], behind_lower, ahead_upper, *across)
     stats = jnp.concatenate([first, second, third], 1).reshape(2, 16, 64)
-    group = np.arange(16, dtype=np.int32)
-    ahead_y, ahead_z = (group // 4 - y) % 4, (group % 4 - z) % 4
-    ahead = jnp.where(c == 0, ahead_z * 4 + ahead_y, ahead_y * 4 + ahead_z)
-    at = jnp.sum(jnp.where(ahead[:, None] == np.arange(16)[None, :], PLACE[None, :], 0), axis=1)
     stats = jnp.take(stats, at, axis=1).reshape(2, 1024)
 
     copies = jnp.broadcast_to(stats, (64, 2, 1024))

time: 120 us -> 119 us (level)
  waiting for transfers between devices: 20.4 us -> 18.2 us
    ppermute x9, waiting for transfers between devices: 10.4 us -> 8.23 us  [shifted(): return lax.ppermute(block, EVERY, crossed_pairs(first, step))]
  transfers between devices with their start and end apart: 15 -> 15, of which waited for: 7 -> 7; matrix products, arithmetic and copies ran while one was open for 4% -> 3% of each run, Pallas kernels for 22% -> 24%
where the time goes in v4:
time: 119 us; the launch traced here: 118 us
  Pallas kernels  48.7 us (41%)
  starting transfers between devices  22.1 us (19%)
  blocking collectives  18.4 us (15%)
  waiting for transfers between devices  18.2 us (15%)
  local copies, waits for them, and re-layouts  4.94 us (4%)
  between operations  2.78 us (2%)
  other arithmetic  2.56 us (2%)
    pallas_call x3, Pallas kernels, chunk_stats(): pl.pallas_call(functools.partial(stats_kernel, counts=counts), in_specs=[...  48.7 us
    all_to_all x1, blocking collectives, body(): lax.all_to_all(copies, CHIPS, split_axis=0, concat_axis=0, tiled=True)  18.4 us
    ppermute x9, starting transfers between devices, shifted(): return lax.ppermute(block, EVERY, crossed_pairs(first, step))  17.2 us
    ppermute x9, waiting for transfers between devices, shifted(): return lax.ppermute(block, EVERY, crossed_pairs(first, step))  8.23 us
    ppermute x3, waiting for transfers between devices, body(): lax.ppermute(half, X, ring_pairs(s))  7.31 us
    ppermute x3, starting transfers between devices, body(): lax.ppermute(half, X, ring_pairs(s))  4.61 us
  transfers between devices with their start and end apart: 15, of which 7 were waited for; matrix products, arithmetic and copies ran while one was open for 3% of the time, Pallas kernels for 24%

profile of v4, /device:TPU:0, one launch (start us, length us, event | category | flops | bytes accessed | tf_op | source)
XLA Modules:
  0.0 117.6 jit_solution(10596839962512930287)
XLA Ops:
  0.7 1.5 %collective-permute-done = bf16[448,128]{1,0:T(8,128)(2,1)S(1)} collective-permute-done((bf16[448,128]{1,0:T(8,128)(2,1)}, bf16[448,128]{1,0:T(8,128)(2,1)S(1)}, u32[]{:S(2)}, u32[]{:S(2)}) %collective-permute-start) | collective-permute-done | bytes 114720 | tf_op jit(solution)/shard_map/ppermute | solution.py:164
  2.2 0.2 collective-permute-start.9
  2.4 1.1 fusion.14
  3.7 2.9 %collective-permute-start.1 = (bf16[448,128]{1,0:T(8,128)(2,1)S(1)}, bf16[448,128]{1,0:T(8,128)(2,1)S(1)}, u32[]{:S(2)}, u32[]{:S(2)}) collective-permute-start(bf16[448,128]{1,0:T(8,128)(2,1)S(1)} %get-tuple-element.50), channel_id=1, source_target_pairs={{0,6},{2,0},{4,2},{6,4},{1,7},{3,1},{5,3},{7,5},{8,14},{10,8},{12,... | collective-permute-start | bytes 344072 | tf_op jit(solution)/shard_map/ppermute | solution.py:171
  6.6 0.8 collective-permute-start.2
  7.4 0.9 collective-permute-start.3
  8.3 3.7 %collective-permute-done.1 = bf16[448,128]{1,0:T(8,128)(2,1)S(1)} collective-permute-done((bf16[448,128]{1,0:T(8,128)(2,1)S(1)}, bf16[448,128]{1,0:T(8,128)(2,1)S(1)}, u32[]{:S(2)}, u32[]{:S(2)}) %collective-permute-start.1) | collective-permute-done | bytes 114720 | tf_op jit(solution)/shard_map/ppermute | solution.py:171
  12.0 2.1 %collective-permute-done.2 = bf16[448,128]{1,0:T(8,128)(2,1)S(1)} collective-permute-done((bf16[448,128]{1,0:T(8,128)(2,1)S(1)}, bf16[448,128]{1,0:T(8,128)(2,1)S(1)}, u32[]{:S(2)}, u32[]{:S(2)}) %collective-permute-start.2) | collective-permute-done | bytes 114720 | tf_op jit(solution)/shard_map/ppermute | solution.py:171
  14.2 1.5 %collective-permute-done.3 = bf16[448,128]{1,0:T(8,128)(2,1)S(1)} collective-permute-done((bf16[448,128]{1,0:T(8,128)(2,1)S(1)}, bf16[448,128]{1,0:T(8,128)(2,1)S(1)}, u32[]{:S(2)}, u32[]{:S(2)}) %collective-permute-start.3) | collective-permute-done | bytes 114720 | tf_op jit(solution)/shard_map/ppermute | solution.py:171
  15.9 2.0 %collective-permute-start.4 = (bf16[1792,128]{1,0:T(8,128)(2,1)S(1)}, bf16[1792,128]{1,0:T(8,128)(2,1)S(1)}, u32[]{:S(2)}, u32[]{:S(2)}) collective-permute-start(bf16[1792,128]{1,0:T(8,128)(2,1)S(1)} %constant_dynamic-slice_fusion), channel_id=1, source_target_pairs={{0,8},{1,33},{2,10},{3,35},{4,12},{5,37},{6,14},{7,39},{8,16},{9,4... | collective-permute-start | bytes 1376264 | tf_op jit(solution)/shard_map/ppermute | solution.py:48
  17.9 2.2 %collective-permute-start.5 = (bf16[1792,128]{1,0:T(8,128)(2,1)S(1)}, bf16[1792,128]{1,0:T(8,128)(2,1)S(1)}, u32[]{:S(2)}, u32[]{:S(2)}) collective-permute-start(bf16[1792,128]{1,0:T(8,128)(2,1)S(1)} %constant_dynamic-slice_fusion), channel_id=1, source_target_pairs={{0,24},{1,97},{2,26},{3,99},{4,28},{5,101},{6,30},{7,103},{8,0},{9... | collective-permute-start | bytes 1376264 | tf_op jit(solution)/shard_map/ppermute | solution.py:48
  20.1 1.8 %collective-permute-start.6 = (bf16[1792,128]{1,0:T(8,128)(2,1)S(1)}, bf16[1792,128]{1,0:T(8,128)(2,1)}, u32[]{:S(2)}, u32[]{:S(2)}) collective-permute-start(bf16[1792,128]{1,0:T(8,128)(2,1)S(1)} %constant_dynamic-slice_fusion), channel_id=1, source_target_pairs={{0,16},{1,65},{2,18},{3,67},{4,20},{5,69},{6,22},{7,71},{8,24},{9,... | collective-permute-start | bytes 1376264 | tf_op jit(solution)/shard_map/ppermute | solution.py:48
  21.9 4.6 %collective-permute-done.4 = bf16[1792,128]{1,0:T(8,128)(2,1)S(1)} collective-permute-done((bf16[1792,128]{1,0:T(8,128)(2,1)S(1)}, bf16[1792,128]{1,0:T(8,128)(2,1)S(1)}, u32[]{:S(2)}, u32[]{:S(2)}) %collective-permute-start.4) | collective-permute-done | bytes 458784 | tf_op jit(solution)/shard_map/ppermute | solution.py:48
  26.5 1.6 %collective-permute-start.7 = (bf16[3584,128]{1,0:T(8,128)(2,1)S(1)}, bf16[3584,128]{1,0:T(8,128)(2,1)S(1)}, u32[]{:S(2)}, u32[]{:S(2)}) collective-permute-start(bf16[3584,128]{1,0:T(8,128)(2,1)S(1)} %pad_maximum_fusion.refs_0_), channel_id=1, source_target_pairs={{0,32},{1,9},{2,34},{3,11},{4,36},{5,13},{6,38},{7,15},{8,40},{9,1... | collective-permute-start | bytes 2752520 | tf_op jit(solution)/shard_map/ppermute | solution.py:48
  28.2 1.7 %collective-permute-start.11 = (bf16[3584,128]{1,0:T(8,128)(2,1)S(1)}, bf16[3584,128]{1,0:T(8,128)(2,1)}, u32[]{:S(2)}, u32[]{:S(2)}) collective-permute-start(bf16[3584,128]{1,0:T(8,128)(2,1)S(1)} %pad_maximum_fusion.refs_0_), channel_id=1, source_target_pairs={{0,96},{1,25},{2,98},{3,27},{4,100},{5,29},{6,102},{7,31},{8,104},... | collective-permute-start | bytes 2752520 | tf_op jit(solution)/shard_map/ppermute | solution.py:48
  30.0 0.6 gather_fusion
  30.8 0.2 select_reduce_fusion.1
  31.0 3.6 %collective-permute-done.6 = bf16[1792,128]{1,0:T(8,128)(2,1)} collective-permute-done((bf16[1792,128]{1,0:T(8,128)(2,1)S(1)}, bf16[1792,128]{1,0:T(8,128)(2,1)}, u32[]{:S(2)}, u32[]{:S(2)}) %collective-permute-start.6) | collective-permute-done | bytes 458784 | tf_op jit(solution)/shard_map/ppermute | solution.py:48
  34.7 1.1 constant_dynamic-update-slice_fusion.7.refs_1_
  35.7 4.4 %collective-permute-start.8 = (bf16[3584,128]{1,0:T(8,128)(2,1)S(1)}, bf16[3584,128]{1,0:T(8,128)(2,1)}, u32[]{:S(2)}, u32[]{:S(2)}) collective-permute-start(bf16[3584,128]{1,0:T(8,128)(2,1)S(1)} %constant_dynamic-update-slice_fusion.7.refs_1_), channel_id=1, source_target_pairs={{0,96},{1,25},{2,98},{3,27},{4,100},{5,29},{6,102},{7,31},{8,104},... | collective-permute-start | bytes 2752520 | tf_op jit(solution)/shard_map/ppermute | solution.py:48
  40.3 14.0 %shard_map.139 = f32[2,256]{1,0:T(2,128)S(1)} custom-call(s32[2,256]{1,0:T(2,128)S(1)} %get-tuple-element.59.local_ids, bf16[3584,128]{1,0:T(8,128)(2,1)S(1)} %pad_maximum_fusion.refs_0_, bf16[3584,128]{1,0:T(8,128)(2,1)S(1)} %constant_dynamic-update-slice_fusion.7.refs_1_, bf16[2000,3584]{1,0:T(8,128)(2,1)} %bitcast.12, ...), custom_call_target="tpu_custom_call" | custom-call | flops 7340032000 | bytes 28672000 | tf_op jit(solution)/shard_map/pallas_call | solution.py:139
  54.3 0.6 collective-permute-start.12
  55.0 2.9 %collective-permute-start.13 = (bf16[3584,128]{1,0:T(8,128)(2,1)}, bf16[3584,128]{1,0:T(8,128)(2,1)S(1)}, u32[]{:S(2)}, u32[]{:S(2)}) collective-permute-start(bf16[3584,128]{1,0:T(8,128)(2,1)} %collective-permute-done.8.refs_1_), channel_id=1, source_target_pairs={{0,96},{1,25},{2,98},{3,27},{4,100},{5,29},{6,102},{7,31},{8,104},... | collective-permute-start | bytes 2752520 | tf_op jit(solution)/shard_map/ppermute | solution.py:48
  57.9 14.1 %shard_map.140 = f32[2,256]{1,0:T(2,128)S(1)} custom-call(s32[2,256]{1,0:T(2,128)S(1)} %get-tuple-element.58.local_ids, bf16[3584,128]{1,0:T(8,128)(2,1)S(1)} %collective-permute-done.7.refs_0_, bf16[3584,128]{1,0:T(8,128)(2,1)} %collective-permute-done.8.refs_1_, bf16[2000,3584]{1,0:T(8,128)(2,1)} %bitcast.13, ...), custom_call_target="tpu_custom_call" | custom-call | flops 7340032000 | bytes 28672000 | tf_op jit(solution)/shard_map/pallas_call | solution.py:139
  72.0 20.6 %shard_map.141 = f32[2,512]{1,0:T(2,128)S(1)} custom-call(s32[2,512]{1,0:T(2,128)S(1)} %slice.34.local_ids, bf16[3584,128]{1,0:T(8,128)(2,1)} %collective-permute-done.10.refs_0_, bf16[3584,128]{1,0:T(8,128)(2,1)} %collective-permute-done.11.refs_1_, bf16[3584,128]{1,0:T(8,128)(2,1)S(1)} %collective-permute-done.12.refs_2_, ...), custom_call_target="tpu_custom_call" | custom-call | flops 14680064000 | bytes 28672000 | tf_op jit(solution)/shard_map/pallas_call | solution.py:139
  92.8 0.6 gather_fusion.1
  93.6 18.4 %all_to_all.5 = f32[64,2,1024]{2,1,0:T(2,128)S(1)} all-to-all(f32[64,2,1024]{2,1,0:T(2,128)S(1)} %broadcast_in_dim.87), channel_id=1, replica_groups=mesh['tok_0'=4,'tok_1'=4,'voc_0'=4,'voc_1'=2] {'tok_0','tok_1','voc_0'}, dimensions={0} | all-to-all | bytes 1048576 | tf_op jit(solution)/shard_map/all_to_all | solution.py:203
  112.0 0.5 slice_reduce_fusion.1
  112.7 1.1 collective-permute-done.14
  113.9 0.2 select_reduce_fusion
  114.2 1.1 fusion.13
  116.0 0.5 dynamic-slice_bitcast_fusion
  (68 shorter events, 1.8 us)
Async XLA Ops:
  0.6 1.6 %collective-permute-start = (bf16[448,128]{1,0:T(8,128)(2,1)}, bf16[448,128]{1,0:T(8,128)(2,1)S(1)}, u32[]{:S(2)}, u32[]{:S(2)}) collective-permute-start(bf16[448,128]{1,0:T(8,128)(2,1)} %bitcast.15), channel_id=1, source_target_pairs={{0,1},{1,0},{2,3},{3,2},{4,5},{5,4},{6,7},{7,6},{8,9},{9,8},{10,11... | collective-permute-start | bytes 344072 | tf_op jit(solution)/shard_map/ppermute | solution.py:164
  2.2 38.0 %collective-permute-start.9 = (bf16[2000,3584]{1,0:T(8,128)(2,1)}, bf16[2000,3584]{1,0:T(8,128)(2,1)}, u32[]{:S(2)}, u32[]{:S(2)}) collective-permute-start(bf16[2000,3584]{1,0:T(8,128)(2,1)} %bitcast.11), channel_id=1, source_target_pairs={{0,1},{1,0},{2,3},{3,2},{4,5},{5,4},{6,7},{7,6},{8,9},{9,8},{10,11... | collective-permute-start | bytes 43008008 | tf_op jit(solution)/shard_map/ppermute | solution.py:166
  3.7 8.3 %collective-permute-start.1 = (bf16[448,128]{1,0:T(8,128)(2,1)S(1)}, bf16[448,128]{1,0:T(8,128)(2,1)S(1)}, u32[]{:S(2)}, u32[]{:S(2)}) collective-permute-start(bf16[448,128]{1,0:T(8,128)(2,1)S(1)} %get-tuple-element.50), channel_id=1, source_target_pairs={{0,6},{2,0},{4,2},{6,4},{1,7},{3,1},{5,3},{7,5},{8,14},{10,8},{12,... | collective-permute-start | bytes 344072 | tf_op jit(solution)/shard_map/ppermute | solution.py:171
  6.6 7.5 %collective-permute-start.2 = (bf16[448,128]{1,0:T(8,128)(2,1)S(1)}, bf16[448,128]{1,0:T(8,128)(2,1)S(1)}, u32[]{:S(2)}, u32[]{:S(2)}) collective-permute-start(bf16[448,128]{1,0:T(8,128)(2,1)S(1)} %get-tuple-element.50), channel_id=1, source_target_pairs={{0,4},{2,6},{4,0},{6,2},{1,5},{3,7},{5,1},{7,3},{8,12},{10,14},{12... | collective-permute-start | bytes 344072 | tf_op jit(solution)/shard_map/ppermute | solution.py:171
  7.4 8.3 %collective-permute-start.3 = (bf16[448,128]{1,0:T(8,128)(2,1)S(1)}, bf16[448,128]{1,0:T(8,128)(2,1)S(1)}, u32[]{:S(2)}, u32[]{:S(2)}) collective-permute-start(bf16[448,128]{1,0:T(8,128)(2,1)S(1)} %get-tuple-element.50), channel_id=1, source_target_pairs={{0,2},{2,4},{4,6},{6,0},{1,3},{3,5},{5,7},{7,1},{8,10},{10,12},{12... | collective-permute-start | bytes 344072 | tf_op jit(solution)/shard_map/ppermute | solution.py:171
  14.2 15.7 %copy-start = (s32[2048]{0:T(1024)S(1)}, s32[2048]{0:T(1024)}, u32[]{:S(2)}) copy-start(s32[2048]{0:T(1024)} %param.14) | copy-start | bytes 24580
  14.2 15.7 %copy-start.6 = (s32[16]{0:T(128)S(1)}, s32[16]{0:T(128)}, u32[]{:S(2)}) copy-start(s32[16]{0:T(128)} %constant.140.clone) | copy-start | bytes 196
  14.2 15.7 %copy-start.7 = (s32[16]{0:T(128)S(1)}, s32[16]{0:T(128)}, u32[]{:S(2)}) copy-start(s32[16]{0:T(128)} %constant.141.clone) | copy-start | bytes 196
  15.7 15.0 %copy-start.4 = (s32[16]{0:T(128)S(1)}, s32[16]{0:T(128)}, u32[]{:S(2)}) copy-start(s32[16]{0:T(128)} %constant.142.clone) | copy-start | bytes 196
  15.8 15.0 %copy-start.5 = (s32[16]{0:T(128)S(1)}, s32[16]{0:T(128)}, u32[]{:S(2)}) copy-start(s32[16]{0:T(128)} %constant.143.clone) | copy-start | bytes 196
  15.8 15.0 %copy-start.8 = (s32[16]{0:T(128)S(1)}, s32[16]{0:T(128)}, u32[]{:S(2)}) copy-start(s32[16]{0:T(128)} %constant.148) | copy-start | bytes 196
  15.9 10.6 %collective-permute-start.4 = (bf16[1792,128]{1,0:T(8,128)(2,1)S(1)}, bf16[1792,128]{1,0:T(8,128)(2,1)S(1)}, u32[]{:S(2)}, u32[]{:S(2)}) collective-permute-start(bf16[1792,128]{1,0:T(8,128)(2,1)S(1)} %constant_dynamic-slice_fusion), channel_id=1, source_target_pairs={{0,8},{1,33},{2,10},{3,35},{4,12},{5,37},{6,14},{7,39},{8,16},{9,4... | collective-permute-start | bytes 1376264 | tf_op jit(solution)/shard_map/ppermute | solution.py:48
  17.9 13.1 %collective-permute-start.5 = (bf16[1792,128]{1,0:T(8,128)(2,1)S(1)}, bf16[1792,128]{1,0:T(8,128)(2,1)S(1)}, u32[]{:S(2)}, u32[]{:S(2)}) collective-permute-start(bf16[1792,128]{1,0:T(8,128)(2,1)S(1)} %constant_dynamic-slice_fusion), channel_id=1, source_target_pairs={{0,24},{1,97},{2,26},{3,99},{4,28},{5,101},{6,30},{7,103},{8,0},{9... | collective-permute-start | bytes 1376264 | tf_op jit(solution)/shard_map/ppermute | solution.py:48
  20.1 14.5 %collective-permute-start.6 = (bf16[1792,128]{1,0:T(8,128)(2,1)S(1)}, bf16[1792,128]{1,0:T(8,128)(2,1)}, u32[]{:S(2)}, u32[]{:S(2)}) collective-permute-start(bf16[1792,128]{1,0:T(8,128)(2,1)S(1)} %constant_dynamic-slice_fusion), channel_id=1, source_target_pairs={{0,16},{1,65},{2,18},{3,67},{4,20},{5,69},{6,22},{7,71},{8,24},{9,... | collective-permute-start | bytes 1376264 | tf_op jit(solution)/shard_map/ppermute | solution.py:48
  26.5 27.8 %collective-permute-start.7 = (bf16[3584,128]{1,0:T(8,128)(2,1)S(1)}, bf16[3584,128]{1,0:T(8,128)(2,1)S(1)}, u32[]{:S(2)}, u32[]{:S(2)}) collective-permute-start(bf16[3584,128]{1,0:T(8,128)(2,1)S(1)} %pad_maximum_fusion.refs_0_), channel_id=1, source_target_pairs={{0,32},{1,9},{2,34},{3,11},{4,36},{5,13},{6,38},{7,15},{8,40},{9,1... | collective-permute-start | bytes 2752520 | tf_op jit(solution)/shard_map/ppermute | solution.py:48
  28.2 43.8 %collective-permute-start.11 = (bf16[3584,128]{1,0:T(8,128)(2,1)S(1)}, bf16[3584,128]{1,0:T(8,128)(2,1)}, u32[]{:S(2)}, u32[]{:S(2)}) collective-permute-start(bf16[3584,128]{1,0:T(8,128)(2,1)S(1)} %pad_maximum_fusion.refs_0_), channel_id=1, source_target_pairs={{0,96},{1,25},{2,98},{3,27},{4,100},{5,29},{6,102},{7,31},{8,104},... | collective-permute-start | bytes 2752520 | tf_op jit(solution)/shard_map/ppermute | solution.py:48
  35.7 18.6 %collective-permute-start.8 = (bf16[3584,128]{1,0:T(8,128)(2,1)S(1)}, bf16[3584,128]{1,0:T(8,128)(2,1)}, u32[]{:S(2)}, u32[]{:S(2)}) collective-permute-start(bf16[3584,128]{1,0:T(8,128)(2,1)S(1)} %constant_dynamic-update-slice_fusion.7.refs_1_), channel_id=1, source_target_pairs={{0,96},{1,25},{2,98},{3,27},{4,100},{5,29},{6,102},{7,31},{8,104},... | collective-permute-start | bytes 2752520 | tf_op jit(solution)/shard_map/ppermute | solution.py:48
  40.1 31.9 %collective-permute-start.10 = (bf16[3584,128]{1,0:T(8,128)(2,1)S(1)}, bf16[3584,128]{1,0:T(8,128)(2,1)}, u32[]{:S(2)}, u32[]{:S(2)}) collective-permute-start(bf16[3584,128]{1,0:T(8,128)(2,1)S(1)} %constant_dynamic-update-slice_fusion.7.refs_1_), channel_id=1, source_target_pairs={{0,32},{1,9},{2,34},{3,11},{4,36},{5,13},{6,38},{7,15},{8,40},{9,1... | collective-permute-start | bytes 2752520 | tf_op jit(solution)/shard_map/ppermute | solution.py:48
  54.3 17.7 %collective-permute-start.12 = (bf16[3584,128]{1,0:T(8,128)(2,1)S(1)}, bf16[3584,128]{1,0:T(8,128)(2,1)S(1)}, u32[]{:S(2)}, u32[]{:S(2)}) collective-permute-start(bf16[3584,128]{1,0:T(8,128)(2,1)S(1)} %collective-permute-done.7.refs_0_), channel_id=1, source_target_pairs={{0,32},{1,9},{2,34},{3,11},{4,36},{5,13},{6,38},{7,15},{8,40},{9,1... | collective-permute-start | bytes 2752520 | tf_op jit(solution)/shard_map/ppermute | solution.py:48
  55.0 17.1 %collective-permute-start.13 = (bf16[3584,128]{1,0:T(8,128)(2,1)}, bf16[3584,128]{1,0:T(8,128)(2,1)S(1)}, u32[]{:S(2)}, u32[]{:S(2)}) collective-permute-start(bf16[3584,128]{1,0:T(8,128)(2,1)} %collective-permute-done.8.refs_1_), channel_id=1, source_target_pairs={{0,96},{1,25},{2,98},{3,27},{4,100},{5,29},{6,102},{7,31},{8,104},... | collective-permute-start | bytes 2752520 | tf_op jit(solution)/shard_map/ppermute | solution.py:48
  92.6 20.1 %copy-start.3 = (s32[16]{0:T(128)S(1)}, s32[16]{0:T(128)}, u32[]{:S(2)}) copy-start(s32[16]{0:T(128)} %param.15) | copy-start | bytes 196
  92.6 21.2 %copy-start.1 = (s32[16]{0:T(128)S(1)}, s32[16]{0:T(128)}, u32[]{:S(2)}) copy-start(s32[16]{0:T(128)} %param.16) | copy-start | bytes 196
  92.6 21.4 %copy-start.2 = (f32[16]{0:T(128)S(1)}, f32[16]{0:T(128)}, u32[]{:S(2)}) copy-start(f32[16]{0:T(128)} %param.17) | copy-start | bytes 196
  112.7 1.2 %collective-permute-start.14 = (f32[16,64]{1,0:T(8,128)S(1)}, f32[16,64]{1,0:T(8,128)S(1)}, u32[]{:S(2)}, u32[]{:S(2)}) collective-permute-start(f32[16,64]{1,0:T(8,128)S(1)} %sub.86), channel_id=1, source_target_pairs={{0,1},{1,0},{2,3},{3,2},{4,5},{5,4},{6,7},{7,6},{8,9},{9,8},{10,11... | collective-permute-start | bytes 12296 | tf_op jit(solution)/shard_map/ppermute | solution.py:207

commit v5 on v4

--- a/solution.py
+++ b/solution.py
@@ -84,7 +84,11 @@
     ]
     for copy in staging:
         copy.start()
+    ahead = 2 if width <= 256 else 1
     bringing(0, 0).start()
+    for i in range(1, ahead):
+        bringing(1, i - 1).start()
+        bringing(0, i).start()
 
     waited = 0
     for p in range(sum(counts) // 2):
@@ -92,7 +96,7 @@
             staging[waited].wait()
             waited += 1
         if p == 0:
-            bringing(1, 0).start()
+            bringing(1, ahead - 1).start()
         lanes = slice(p * 128, (p + 1) * 128)
         for x in range(4):
             at = 2 * p * ROWS + x * 448
@@ -104,10 +108,10 @@
     picked[...] = jnp.zeros_like(picked)
 
     def step(i, carry):
-        @pl.when(i + 1 < steps)
+        @pl.when(i + ahead < steps)
         def _():
-            bringing(0, i + 1).start()
-            bringing(1, i + 1).start()
+            bringing(0, i + ahead).start()
+            bringing(1, i + ahead).start()
 
         bringing(0, i).wait()
         bringing(1, i).wait()
@@ -189,7 +193,8 @@
     upper = jnp.concatenate([own, a_behind], 0)
     lower = jnp.concatenate([a_ahead, *a_across], 0)
     behind_upper, ahead_lower = shifted(upper, False, 1), shifted(lower, False, 3)
-    behind_lower, ahead_upper = shifted(lower, False, 1), shifted(upper, False, 3)
+    upper_later, lower = lax.optimization_barrier((upper, lower))
+    behind_lower, ahead_upper = shifted(lower, False, 1), shifted(upper_later, False, 3)
     first = chunk_stats(weights, local_ids[:, :256], upper, lower)
     behind_upper, ahead_lower, first = lax.optimization_barrier((behind_upper, ahead_lower, first))
     across = [shifted(behind_upper, False, 1), shifted(ahead_lower, False, 3)]

time: 119 us -> 116 us (0.975)
  waiting for transfers between devices: 18.2 us -> 22.8 us
  Pallas kernels: 48.7 us -> 45 us
  blocking collectives: 18.4 us -> 16.2 us
  starting transfers between devices: 22.1 us -> 20.6 us
    ppermute x9, waiting for transfers between devices: 8.23 us -> 12.7 us  [shifted(): return lax.ppermute(block, EVERY, crossed_pairs(first, step))]
    pallas_call x3, Pallas kernels: 48.7 us -> 45 us  [chunk_stats(): pl.pallas_call(functools.partial(stats_kernel, counts=counts), in_specs=[...]
    all_to_all x1, blocking collectives: 18.4 us -> 16.2 us  [body(): lax.all_to_all(copies, CHIPS, split_axis=0, concat_axis=0, tiled=True)]
    ppermute x9, starting transfers between devices: 17.2 us -> 15.7 us  [shifted(): return lax.ppermute(block, EVERY, crossed_pairs(first, step))]
  transfers between devices with their start and end apart: 15 -> 15, of which waited for: 7 -> 9; matrix products, arithmetic and copies ran while one was open for 3% -> 3% of each run, Pallas kernels for 24% -> 21%
where the time goes in v5:
time: 116 us; the launch traced here: 115 us
  Pallas kernels  45 us (39%)
  waiting for transfers between devices  22.8 us (20%)
  starting transfers between devices  20.6 us (18%)
  blocking collectives  16.2 us (14%)
  local copies, waits for them, and re-layouts  3.92 us (3%)
  other arithmetic  3.57 us (3%)
  between operations  2.79 us (2%)
    pallas_call x3, Pallas kernels, chunk_stats(): pl.pallas_call(functools.partial(stats_kernel, counts=counts), in_specs=[...  45 us
    all_to_all x1, blocking collectives, body(): lax.all_to_all(copies, CHIPS, split_axis=0, concat_axis=0, tiled=True)  16.2 us
    ppermute x9, starting transfers between devices, shifted(): return lax.ppermute(block, EVERY, crossed_pairs(first, step))  15.7 us
    ppermute x9, waiting for transfers between devices, shifted(): return lax.ppermute(block, EVERY, crossed_pairs(first, step))  12.7 us
    ppermute x3, waiting for transfers between devices, body(): lax.ppermute(half, X, ring_pairs(s))  7.35 us
    ppermute x3, starting transfers between devices, body(): lax.ppermute(half, X, ring_pairs(s))  4.61 us
  transfers between devices with their start and end apart: 15, of which 9 were waited for; matrix products, arithmetic and copies ran while one was open for 3% of the time, Pallas kernels for 21%

profile of v5, /device:TPU:0, one launch (start us, length us, event | category | flops | bytes accessed | tf_op | source)
XLA Modules:
  0.0 114.9 jit_solution(5645522445872300470)
XLA Ops:
  0.7 1.5 %collective-permute-done = bf16[448,128]{1,0:T(8,128)(2,1)S(1)} collective-permute-done((bf16[448,128]{1,0:T(8,128)(2,1)}, bf16[448,128]{1,0:T(8,128)(2,1)S(1)}, u32[]{:S(2)}, u32[]{:S(2)}) %collective-permute-start) | collective-permute-done | bytes 114720 | tf_op jit(solution)/shard_map/ppermute | solution.py:168
  2.4 1.1 fusion.14
  3.8 2.9 %collective-permute-start.1 = (bf16[448,128]{1,0:T(8,128)(2,1)S(1)}, bf16[448,128]{1,0:T(8,128)(2,1)S(1)}, u32[]{:S(2)}, u32[]{:S(2)}) collective-permute-start(bf16[448,128]{1,0:T(8,128)(2,1)S(1)} %get-tuple-element.54), channel_id=1, source_target_pairs={{0,6},{2,0},{4,2},{6,4},{1,7},{3,1},{5,3},{7,5},{8,14},{10,8},{12,... | collective-permute-start | bytes 344072 | tf_op jit(solution)/shard_map/ppermute | solution.py:175
  6.7 0.8 collective-permute-start.2
  7.5 0.9 collective-permute-start.3
  8.4 3.7 %collective-permute-done.1 = bf16[448,128]{1,0:T(8,128)(2,1)S(1)} collective-permute-done((bf16[448,128]{1,0:T(8,128)(2,1)S(1)}, bf16[448,128]{1,0:T(8,128)(2,1)S(1)}, u32[]{:S(2)}, u32[]{:S(2)}) %collective-permute-start.1) | collective-permute-done | bytes 114720 | tf_op jit(solution)/shard_map/ppermute | solution.py:175
  12.1 2.1 %collective-permute-done.2 = bf16[448,128]{1,0:T(8,128)(2,1)S(1)} collective-permute-done((bf16[448,128]{1,0:T(8,128)(2,1)S(1)}, bf16[448,128]{1,0:T(8,128)(2,1)S(1)}, u32[]{:S(2)}, u32[]{:S(2)}) %collective-permute-start.2) | collective-permute-done | bytes 114720 | tf_op jit(solution)/shard_map/ppermute | solution.py:175
  14.2 1.5 %collective-permute-done.3 = bf16[448,128]{1,0:T(8,128)(2,1)S(1)} collective-permute-done((bf16[448,128]{1,0:T(8,128)(2,1)S(1)}, bf16[448,128]{1,0:T(8,128)(2,1)S(1)}, u32[]{:S(2)}, u32[]{:S(2)}) %collective-permute-start.3) | collective-permute-done | bytes 114720 | tf_op jit(solution)/shard_map/ppermute | solution.py:175
  15.9 2.0 %collective-permute-start.4 = (bf16[1792,128]{1,0:T(8,128)(2,1)S(1)}, bf16[1792,128]{1,0:T(8,128)(2,1)S(1)}, u32[]{:S(2)}, u32[]{:S(2)}) collective-permute-start(bf16[1792,128]{1,0:T(8,128)(2,1)S(1)} %constant_dynamic-slice_fusion), channel_id=1, source_target_pairs={{0,8},{1,33},{2,10},{3,35},{4,12},{5,37},{6,14},{7,39},{8,16},{9,4... | collective-permute-start | bytes 1376264 | tf_op jit(solution)/shard_map/ppermute | solution.py:48
  17.9 2.2 %collective-permute-start.5 = (bf16[1792,128]{1,0:T(8,128)(2,1)S(1)}, bf16[1792,128]{1,0:T(8,128)(2,1)S(1)}, u32[]{:S(2)}, u32[]{:S(2)}) collective-permute-start(bf16[1792,128]{1,0:T(8,128)(2,1)S(1)} %constant_dynamic-slice_fusion), channel_id=1, source_target_pairs={{0,24},{1,97},{2,26},{3,99},{4,28},{5,101},{6,30},{7,103},{8,0},{9... | collective-permute-start | bytes 1376264 | tf_op jit(solution)/shard_map/ppermute | solution.py:48
  20.1 1.8 %collective-permute-start.6 = (bf16[1792,128]{1,0:T(8,128)(2,1)S(1)}, bf16[1792,128]{1,0:T(8,128)(2,1)S(1)}, u32[]{:S(2)}, u32[]{:S(2)}) collective-permute-start(bf16[1792,128]{1,0:T(8,128)(2,1)S(1)} %constant_dynamic-slice_fusion), channel_id=1, source_target_pairs={{0,16},{1,65},{2,18},{3,67},{4,20},{5,69},{6,22},{7,71},{8,24},{9,... | collective-permute-start | bytes 1376264 | tf_op jit(solution)/shard_map/ppermute | solution.py:48
  21.9 4.6 %collective-permute-done.4 = bf16[1792,128]{1,0:T(8,128)(2,1)S(1)} collective-permute-done((bf16[1792,128]{1,0:T(8,128)(2,1)S(1)}, bf16[1792,128]{1,0:T(8,128)(2,1)S(1)}, u32[]{:S(2)}, u32[]{:S(2)}) %collective-permute-start.4) | collective-permute-done | bytes 458784 | tf_op jit(solution)/shard_map/ppermute | solution.py:48
  26.6 0.6 gather_fusion
  27.5 0.2 select_reduce_fusion.1
  27.7 3.4 %collective-permute-done.5 = bf16[1792,128]{1,0:T(8,128)(2,1)S(1)} collective-permute-done((bf16[1792,128]{1,0:T(8,128)(2,1)S(1)}, bf16[1792,128]{1,0:T(8,128)(2,1)S(1)}, u32[]{:S(2)}, u32[]{:S(2)}) %collective-permute-start.5) | collective-permute-done | bytes 458784 | tf_op jit(solution)/shard_map/ppermute | solution.py:48
  31.1 1.8 %collective-permute-done.6 = bf16[1792,128]{1,0:T(8,128)(2,1)S(1)} collective-permute-done((bf16[1792,128]{1,0:T(8,128)(2,1)S(1)}, bf16[1792,128]{1,0:T(8,128)(2,1)S(1)}, u32[]{:S(2)}, u32[]{:S(2)}) %collective-permute-start.6) | collective-permute-done | bytes 458784 | tf_op jit(solution)/shard_map/ppermute | solution.py:48
  33.0 3.1 %collective-permute-start.8 = (bf16[3584,128]{1,0:T(8,128)(2,1)S(1)}, bf16[3584,128]{1,0:T(8,128)(2,1)S(1)}, u32[]{:S(2)}, u32[]{:S(2)}) collective-permute-start(bf16[3584,128]{1,0:T(8,128)(2,1)S(1)} %constant_dynamic-update-slice_fusion.7.refs_1_), channel_id=1, source_target_pairs={{0,96},{1,25},{2,98},{3,27},{4,100},{5,29},{6,102},{7,31},{8,104},... | collective-permute-start | bytes 2752520 | tf_op jit(solution)/shard_map/ppermute | solution.py:48
  36.1 1.1 pad_maximum_fusion.refs_0_
  37.2 0.6 collective-permute-start.10
  37.8 2.7 %collective-permute-start.11 = (bf16[3584,128]{1,0:T(8,128)(2,1)S(1)}, bf16[3584,128]{1,0:T(8,128)(2,1)}, u32[]{:S(2)}, u32[]{:S(2)}) collective-permute-start(bf16[3584,128]{1,0:T(8,128)(2,1)S(1)} %pad_maximum_fusion.refs_0_), channel_id=1, source_target_pairs={{0,96},{1,25},{2,98},{3,27},{4,100},{5,29},{6,102},{7,31},{8,104},... | collective-permute-start | bytes 2752520 | tf_op jit(solution)/shard_map/ppermute | solution.py:48
  40.7 12.3 %shard_map.139 = f32[2,256]{1,0:T(2,128)S(1)} custom-call(s32[2,256]{1,0:T(2,128)S(1)} %get-tuple-element.63.local_ids, bf16[3584,128]{1,0:T(8,128)(2,1)S(1)} %pad_maximum_fusion.refs_0_, bf16[3584,128]{1,0:T(8,128)(2,1)S(1)} %constant_dynamic-update-slice_fusion.7.refs_1_, bf16[2000,3584]{1,0:T(8,128)(2,1)} %bitcast.12, ...), custom_call_target="tpu_custom_call" | custom-call | flops 7340032000 | bytes 28672000 | tf_op jit(solution)/shard_map/pallas_call | solution.py:143
  53.1 3.2 %collective-permute-start.13 = (bf16[3584,128]{1,0:T(8,128)(2,1)S(1)}, bf16[3584,128]{1,0:T(8,128)(2,1)S(1)}, u32[]{:S(2)}, u32[]{:S(2)}) collective-permute-start(bf16[3584,128]{1,0:T(8,128)(2,1)S(1)} %collective-permute-done.8.refs_1_), channel_id=1, source_target_pairs={{0,96},{1,25},{2,98},{3,27},{4,100},{5,29},{6,102},{7,31},{8,104},... | collective-permute-start | bytes 2752520 | tf_op jit(solution)/shard_map/ppermute | solution.py:48
  56.3 12.2 %shard_map.140 = f32[2,256]{1,0:T(2,128)S(1)} custom-call(s32[2,256]{1,0:T(2,128)S(1)} %get-tuple-element.62.local_ids, bf16[3584,128]{1,0:T(8,128)(2,1)} %collective-permute-done.7.refs_0_, bf16[3584,128]{1,0:T(8,128)(2,1)S(1)} %collective-permute-done.8.refs_1_, bf16[2000,3584]{1,0:T(8,128)(2,1)} %bitcast.13, ...), custom_call_target="tpu_custom_call" | custom-call | flops 7340032000 | bytes 28672000 | tf_op jit(solution)/shard_map/pallas_call | solution.py:143
  68.5 2.9 %collective-permute-done.12.refs_2_ = bf16[3584,128]{1,0:T(8,128)(2,1)S(1)} collective-permute-done((bf16[3584,128]{1,0:T(8,128)(2,1)}, bf16[3584,128]{1,0:T(8,128)(2,1)S(1)}, u32[]{:S(2)}, u32[]{:S(2)}) %collective-permute-start.12) | collective-permute-done | bytes 917536 | tf_op jit(solution)/shard_map/ppermute | solution.py:48
  71.5 20.6 %shard_map.141 = f32[2,512]{1,0:T(2,128)S(1)} custom-call(s32[2,512]{1,0:T(2,128)S(1)} %slice.34.local_ids, bf16[3584,128]{1,0:T(8,128)(2,1)} %collective-permute-done.10.refs_0_, bf16[3584,128]{1,0:T(8,128)(2,1)} %collective-permute-done.11.refs_1_, bf16[3584,128]{1,0:T(8,128)(2,1)S(1)} %collective-permute-done.12.refs_2_, ...), custom_call_target="tpu_custom_call" | custom-call | flops 14680064000 | bytes 28672000 | tf_op jit(solution)/shard_map/pallas_call | solution.py:143
  92.2 0.6 gather_fusion.1
  93.0 16.2 %all_to_all.5 = f32[64,2,1024]{2,1,0:T(2,128)S(1)} all-to-all(f32[64,2,1024]{2,1,0:T(2,128)S(1)} %broadcast_in_dim.87), channel_id=1, replica_groups=mesh['tok_0'=4,'tok_1'=4,'voc_0'=4,'voc_1'=2] {'tok_0','tok_1','voc_0'}, dimensions={0} | all-to-all | bytes 1048576 | tf_op jit(solution)/shard_map/all_to_all | solution.py:208
  109.3 0.5 slice_reduce_fusion.1
  110.0 1.1 collective-permute-done.14
  111.1 0.2 select_reduce_fusion
  111.5 1.1 fusion.13
  113.2 0.5 dynamic-slice_bitcast_fusion
  (70 shorter events, 2.1 us)
Async XLA Ops:
  0.6 1.6 %collective-permute-start = (bf16[448,128]{1,0:T(8,128)(2,1)}, bf16[448,128]{1,0:T(8,128)(2,1)S(1)}, u32[]{:S(2)}, u32[]{:S(2)}) collective-permute-start(bf16[448,128]{1,0:T(8,128)(2,1)} %bitcast.15), channel_id=1, source_target_pairs={{0,1},{1,0},{2,3},{3,2},{4,5},{5,4},{6,7},{7,6},{8,9},{9,8},{10,11... | collective-permute-start | bytes 344072 | tf_op jit(solution)/shard_map/ppermute | solution.py:168
  2.2 38.5 %collective-permute-start.9 = (bf16[2000,3584]{1,0:T(8,128)(2,1)}, bf16[2000,3584]{1,0:T(8,128)(2,1)}, u32[]{:S(2)}, u32[]{:S(2)}) collective-permute-start(bf16[2000,3584]{1,0:T(8,128)(2,1)} %bitcast.11), channel_id=1, source_target_pairs={{0,1},{1,0},{2,3},{3,2},{4,5},{5,4},{6,7},{7,6},{8,9},{9,8},{10,11... | collective-permute-start | bytes 43008008 | tf_op jit(solution)/shard_map/ppermute | solution.py:170
  3.5 23.0 %copy-start.1 = (s32[2048]{0:T(1024)S(1)}, s32[2048]{0:T(1024)}, u32[]{:S(2)}) copy-start(s32[2048]{0:T(1024)} %param.14) | copy-start | bytes 24580
  3.5 23.1 %copy-start.7 = (s32[16]{0:T(128)S(1)}, s32[16]{0:T(128)}, u32[]{:S(2)}) copy-start(s32[16]{0:T(128)} %constant.140.clone) | copy-start | bytes 196
  3.5 23.1 %copy-start.8 = (s32[16]{0:T(128)S(1)}, s32[16]{0:T(128)}, u32[]{:S(2)}) copy-start(s32[16]{0:T(128)} %constant.141.clone) | copy-start | bytes 196
  3.5 23.9 %copy-start.5 = (s32[16]{0:T(128)S(1)}, s32[16]{0:T(128)}, u32[]{:S(2)}) copy-start(s32[16]{0:T(128)} %constant.142.clone) | copy-start | bytes 196
  3.5 23.9 %copy-start.6 = (s32[16]{0:T(128)S(1)}, s32[16]{0:T(128)}, u32[]{:S(2)}) copy-start(s32[16]{0:T(128)} %constant.143.clone) | copy-start | bytes 196
  3.5 24.0 %copy-start.9 = (s32[16]{0:T(128)S(1)}, s32[16]{0:T(128)}, u32[]{:S(2)}) copy-start(s32[16]{0:T(128)} %constant.148) | copy-start | bytes 196
  3.8 8.3 %collective-permute-start.1 = (bf16[448,128]{1,0:T(8,128)(2,1)S(1)}, bf16[448,128]{1,0:T(8,128)(2,1)S(1)}, u32[]{:S(2)}, u32[]{:S(2)}) collective-permute-start(bf16[448,128]{1,0:T(8,128)(2,1)S(1)} %get-tuple-element.54), channel_id=1, source_target_pairs={{0,6},{2,0},{4,2},{6,4},{1,7},{3,1},{5,3},{7,5},{8,14},{10,8},{12,... | collective-permute-start | bytes 344072 | tf_op jit(solution)/shard_map/ppermute | solution.py:175
  6.7 7.5 %collective-permute-start.2 = (bf16[448,128]{1,0:T(8,128)(2,1)S(1)}, bf16[448,128]{1,0:T(8,128)(2,1)S(1)}, u32[]{:S(2)}, u32[]{:S(2)}) collective-permute-start(bf16[448,128]{1,0:T(8,128)(2,1)S(1)} %get-tuple-element.54), channel_id=1, source_target_pairs={{0,4},{2,6},{4,0},{6,2},{1,5},{3,7},{5,1},{7,3},{8,12},{10,14},{12... | collective-permute-start | bytes 344072 | tf_op jit(solution)/shard_map/ppermute | solution.py:175
  7.5 8.3 %collective-permute-start.3 = (bf16[448,128]{1,0:T(8,128)(2,1)S(1)}, bf16[448,128]{1,0:T(8,128)(2,1)S(1)}, u32[]{:S(2)}, u32[]{:S(2)}) collective-permute-start(bf16[448,128]{1,0:T(8,128)(2,1)S(1)} %get-tuple-element.54), channel_id=1, source_target_pairs={{0,2},{2,4},{4,6},{6,0},{1,3},{3,5},{5,7},{7,1},{8,10},{10,12},{12... | collective-permute-start | bytes 344072 | tf_op jit(solution)/shard_map/ppermute | solution.py:175
  15.9 10.6 %collective-permute-start.4 = (bf16[1792,128]{1,0:T(8,128)(2,1)S(1)}, bf16[1792,128]{1,0:T(8,128)(2,1)S(1)}, u32[]{:S(2)}, u32[]{:S(2)}) collective-permute-start(bf16[1792,128]{1,0:T(8,128)(2,1)S(1)} %constant_dynamic-slice_fusion), channel_id=1, source_target_pairs={{0,8},{1,33},{2,10},{3,35},{4,12},{5,37},{6,14},{7,39},{8,16},{9,4... | collective-permute-start | bytes 1376264 | tf_op jit(solution)/shard_map/ppermute | solution.py:48
  17.9 13.2 %collective-permute-start.5 = (bf16[1792,128]{1,0:T(8,128)(2,1)S(1)}, bf16[1792,128]{1,0:T(8,128)(2,1)S(1)}, u32[]{:S(2)}, u32[]{:S(2)}) collective-permute-start(bf16[1792,128]{1,0:T(8,128)(2,1)S(1)} %constant_dynamic-slice_fusion), channel_id=1, source_target_pairs={{0,24},{1,97},{2,26},{3,99},{4,28},{5,101},{6,30},{7,103},{8,0},{9... | collective-permute-start | bytes 1376264 | tf_op jit(solution)/shard_map/ppermute | solution.py:48
  20.1 12.7 %collective-permute-start.6 = (bf16[1792,128]{1,0:T(8,128)(2,1)S(1)}, bf16[1792,128]{1,0:T(8,128)(2,1)S(1)}, u32[]{:S(2)}, u32[]{:S(2)}) collective-permute-start(bf16[1792,128]{1,0:T(8,128)(2,1)S(1)} %constant_dynamic-slice_fusion), channel_id=1, source_target_pairs={{0,16},{1,65},{2,18},{3,67},{4,20},{5,69},{6,22},{7,71},{8,24},{9,... | collective-permute-start | bytes 1376264 | tf_op jit(solution)/shard_map/ppermute | solution.py:48
  26.5 6.4 %copy-start = (bf16[1792,128]{1,0:T(8,128)(2,1)}, bf16[1792,128]{1,0:T(8,128)(2,1)S(1)}, u32[]{:S(2)}) copy-start(bf16[1792,128]{1,0:T(8,128)(2,1)S(1)} %collective-permute-done.4) | copy-start | bytes 1376260
  33.0 20.0 %collective-permute-start.8 = (bf16[3584,128]{1,0:T(8,128)(2,1)S(1)}, bf16[3584,128]{1,0:T(8,128)(2,1)S(1)}, u32[]{:S(2)}, u32[]{:S(2)}) collective-permute-start(bf16[3584,128]{1,0:T(8,128)(2,1)S(1)} %constant_dynamic-update-slice_fusion.7.refs_1_), channel_id=1, source_target_pairs={{0,96},{1,25},{2,98},{3,27},{4,100},{5,29},{6,102},{7,31},{8,104},... | collective-permute-start | bytes 2752520 | tf_op jit(solution)/shard_map/ppermute | solution.py:48
  37.2 15.9 %collective-permute-start.7 = (bf16[3584,128]{1,0:T(8,128)(2,1)S(1)}, bf16[3584,128]{1,0:T(8,128)(2,1)}, u32[]{:S(2)}, u32[]{:S(2)}) collective-permute-start(bf16[3584,128]{1,0:T(8,128)(2,1)S(1)} %pad_maximum_fusion.refs_0_), channel_id=1, source_target_pairs={{0,32},{1,9},{2,34},{3,11},{4,36},{5,13},{6,38},{7,15},{8,40},{9,1... | collective-permute-start | bytes 2752520 | tf_op jit(solution)/shard_map/ppermute | solution.py:48
  37.2 31.3 %collective-permute-start.10 = (bf16[3584,128]{1,0:T(8,128)(2,1)S(1)}, bf16[3584,128]{1,0:T(8,128)(2,1)}, u32[]{:S(2)}, u32[]{:S(2)}) collective-permute-start(bf16[3584,128]{1,0:T(8,128)(2,1)S(1)} %constant_dynamic-update-slice_fusion.7.refs_1_), channel_id=1, source_target_pairs={{0,32},{1,9},{2,34},{3,11},{4,36},{5,13},{6,38},{7,15},{8,40},{9,1... | collective-permute-start | bytes 2752520 | tf_op jit(solution)/shard_map/ppermute | solution.py:48
  37.8 30.7 %collective-permute-start.11 = (bf16[3584,128]{1,0:T(8,128)(2,1)S(1)}, bf16[3584,128]{1,0:T(8,128)(2,1)}, u32[]{:S(2)}, u32[]{:S(2)}) collective-permute-start(bf16[3584,128]{1,0:T(8,128)(2,1)S(1)} %pad_maximum_fusion.refs_0_), channel_id=1, source_target_pairs={{0,96},{1,25},{2,98},{3,27},{4,100},{5,29},{6,102},{7,31},{8,104},... | collective-permute-start | bytes 2752520 | tf_op jit(solution)/shard_map/ppermute | solution.py:48
  53.0 18.5 %collective-permute-start.12 = (bf16[3584,128]{1,0:T(8,128)(2,1)}, bf16[3584,128]{1,0:T(8,128)(2,1)S(1)}, u32[]{:S(2)}, u32[]{:S(2)}) collective-permute-start(bf16[3584,128]{1,0:T(8,128)(2,1)} %collective-permute-done.7.refs_0_), channel_id=1, source_target_pairs={{0,32},{1,9},{2,34},{3,11},{4,36},{5,13},{6,38},{7,15},{8,40},{9,1... | collective-permute-start | bytes 2752520 | tf_op jit(solution)/shard_map/ppermute | solution.py:48
  53.1 18.4 %collective-permute-start.13 = (bf16[3584,128]{1,0:T(8,128)(2,1)S(1)}, bf16[3584,128]{1,0:T(8,128)(2,1)S(1)}, u32[]{:S(2)}, u32[]{:S(2)}) collective-permute-start(bf16[3584,128]{1,0:T(8,128)(2,1)S(1)} %collective-permute-done.8.refs_1_), channel_id=1, source_target_pairs={{0,96},{1,25},{2,98},{3,27},{4,100},{5,29},{6,102},{7,31},{8,104},... | collective-permute-start | bytes 2752520 | tf_op jit(solution)/shard_map/ppermute | solution.py:48
  92.1 17.9 %copy-start.4 = (s32[16]{0:T(128)S(1)}, s32[16]{0:T(128)}, u32[]{:S(2)}) copy-start(s32[16]{0:T(128)} %param.15) | copy-start | bytes 196
  92.1 19.1 %copy-start.2 = (s32[16]{0:T(128)S(1)}, s32[16]{0:T(128)}, u32[]{:S(2)}) copy-start(s32[16]{0:T(128)} %param.16) | copy-start | bytes 196
  92.1 19.2 %copy-start.3 = (f32[16]{0:T(128)S(1)}, f32[16]{0:T(128)}, u32[]{:S(2)}) copy-start(f32[16]{0:T(128)} %param.17) | copy-start | bytes 196
  109.9 1.2 %collective-permute-start.14 = (f32[16,64]{1,0:T(8,128)S(1)}, f32[16,64]{1,0:T(8,128)S(1)}, u32[]{:S(2)}, u32[]{:S(2)}) collective-permute-start(f32[16,64]{1,0:T(8,128)S(1)} %sub.86), channel_id=1, source_target_pairs={{0,1},{1,0},{2,3},{3,2},{4,5},{5,4},{6,7},{7,6},{8,9},{9,8},{10,11... | collective-permute-start | bytes 12296 | tf_op jit(solution)/shard_map/ppermute | solution.py:212

commit v6 on v5

--- a/solution.py
+++ b/solution.py
@@ -177,7 +177,8 @@
     own = lax.dynamic_slice_in_dim(turned, lax.rem(4 - x, 4) * 448, 1792, 0)
 
     a_behind, a_ahead, *a_across = (shifted(own, True, k) for k in (1, 3, 2))
-    a_behind, targets, y, z, c = lax.optimization_barrier((a_behind, targets, y, z, c))
+    upper = jnp.concatenate([own, a_behind], 0)
+    upper, targets, y, z, c = lax.optimization_barrier((upper, targets, y, z, c))
 
     off_y, off_z = jnp.where(c == 0, ALONG_B, ALONG_A), jnp.where(c == 0, ALONG_A, ALONG_B)
     source = (y + off_y) % 4 * 4 + (z + off_z) % 4
@@ -190,7 +191,6 @@
     at = jnp.sum(jnp.where(ahead[:, None] == np.arange(16)[None, :], PLACE[None, :], 0), axis=1)
     a_ahead, a_across, local_ids, at = lax.optimization_barrier((a_ahead, a_across, local_ids, at))
 
-    upper = jnp.concatenate([own, a_behind], 0)
     lower = jnp.concatenate([a_ahead, *a_across], 0)
     behind_upper, ahead_lower = shifted(upper, False, 1), shifted(lower, False, 3)
     upper_later, lower = lax.optimization_barrier((upper, lower))

time: 116 us -> 115 us (level)
  no operation moved by 1% of the time
where the time goes in v6:
time: 115 us; the launch traced here: 114 us
  Pallas kernels  45 us (39%)
  waiting for transfers between devices  22.7 us (20%)
  starting transfers between devices  20.5 us (18%)
  blocking collectives  16.2 us (14%)
  local copies, waits for them, and re-layouts  3.92 us (3%)
  between operations  2.8 us (2%)
  other arithmetic  2.56 us (2%)
    pallas_call x3, Pallas kernels, chunk_stats(): pl.pallas_call(functools.partial(stats_kernel, counts=counts), in_specs=[...  45 us
    all_to_all x1, blocking collectives, body(): lax.all_to_all(copies, CHIPS, split_axis=0, concat_axis=0, tiled=True)  16.2 us
    ppermute x9, starting transfers between devices, shifted(): return lax.ppermute(block, EVERY, crossed_pairs(first, step))  15.6 us
    ppermute x9, waiting for transfers between devices, shifted(): return lax.ppermute(block, EVERY, crossed_pairs(first, step))  12.7 us
    ppermute x3, waiting for transfers between devices, body(): lax.ppermute(half, X, ring_pairs(s))  7.31 us
    ppermute x3, starting transfers between devices, body(): lax.ppermute(half, X, ring_pairs(s))  4.61 us
  transfers between devices with their start and end apart: 15, of which 9 were waited for; matrix products, arithmetic and copies ran while one was open for 3% of the time, Pallas kernels for 21%

profile of v6, /device:TPU:0, one launch (start us, length us, event | category | flops | bytes accessed | tf_op | source)
XLA Modules:
  0.0 113.7 jit_solution(6043386157839136002)
XLA Ops:
  0.7 1.5 %collective-permute-done = bf16[448,128]{1,0:T(8,128)(2,1)S(1)} collective-permute-done((bf16[448,128]{1,0:T(8,128)(2,1)}, bf16[448,128]{1,0:T(8,128)(2,1)S(1)}, u32[]{:S(2)}, u32[]{:S(2)}) %collective-permute-start) | collective-permute-done | bytes 114720 | tf_op jit(solution)/shard_map/ppermute | solution.py:168
  2.2 0.2 collective-permute-start.9
  2.4 1.1 fusion.14
  3.7 2.9 %collective-permute-start.1 = (bf16[448,128]{1,0:T(8,128)(2,1)S(1)}, bf16[448,128]{1,0:T(8,128)(2,1)S(1)}, u32[]{:S(2)}, u32[]{:S(2)}) collective-permute-start(bf16[448,128]{1,0:T(8,128)(2,1)S(1)} %get-tuple-element.54), channel_id=1, source_target_pairs={{0,6},{2,0},{4,2},{6,4},{1,7},{3,1},{5,3},{7,5},{8,14},{10,8},{12,... | collective-permute-start | bytes 344072 | tf_op jit(solution)/shard_map/ppermute | solution.py:175
  6.6 0.8 collective-permute-start.2
  7.4 0.9 collective-permute-start.3
  8.3 3.7 %collective-permute-done.1 = bf16[448,128]{1,0:T(8,128)(2,1)S(1)} collective-permute-done((bf16[448,128]{1,0:T(8,128)(2,1)S(1)}, bf16[448,128]{1,0:T(8,128)(2,1)S(1)}, u32[]{:S(2)}, u32[]{:S(2)}) %collective-permute-start.1) | collective-permute-done | bytes 114720 | tf_op jit(solution)/shard_map/ppermute | solution.py:175
  12.0 2.1 %collective-permute-done.2 = bf16[448,128]{1,0:T(8,128)(2,1)S(1)} collective-permute-done((bf16[448,128]{1,0:T(8,128)(2,1)S(1)}, bf16[448,128]{1,0:T(8,128)(2,1)S(1)}, u32[]{:S(2)}, u32[]{:S(2)}) %collective-permute-start.2) | collective-permute-done | bytes 114720 | tf_op jit(solution)/shard_map/ppermute | solution.py:175
  14.2 1.5 %collective-permute-done.3 = bf16[448,128]{1,0:T(8,128)(2,1)S(1)} collective-permute-done((bf16[448,128]{1,0:T(8,128)(2,1)S(1)}, bf16[448,128]{1,0:T(8,128)(2,1)S(1)}, u32[]{:S(2)}, u32[]{:S(2)}) %collective-permute-start.3) | collective-permute-done | bytes 114720 | tf_op jit(solution)/shard_map/ppermute | solution.py:175
  15.9 2.0 %collective-permute-start.4 = (bf16[1792,128]{1,0:T(8,128)(2,1)S(1)}, bf16[1792,128]{1,0:T(8,128)(2,1)S(1)}, u32[]{:S(2)}, u32[]{:S(2)}) collective-permute-start(bf16[1792,128]{1,0:T(8,128)(2,1)S(1)} %constant_dynamic-slice_fusion), channel_id=1, source_target_pairs={{0,8},{1,33},{2,10},{3,35},{4,12},{5,37},{6,14},{7,39},{8,16},{9,4... | collective-permute-start | bytes 1376264 | tf_op jit(solution)/shard_map/ppermute | solution.py:48
  17.9 2.2 %collective-permute-start.5 = (bf16[1792,128]{1,0:T(8,128)(2,1)S(1)}, bf16[1792,128]{1,0:T(8,128)(2,1)S(1)}, u32[]{:S(2)}, u32[]{:S(2)}) collective-permute-start(bf16[1792,128]{1,0:T(8,128)(2,1)S(1)} %constant_dynamic-slice_fusion), channel_id=1, source_target_pairs={{0,24},{1,97},{2,26},{3,99},{4,28},{5,101},{6,30},{7,103},{8,0},{9... | collective-permute-start | bytes 1376264 | tf_op jit(solution)/shard_map/ppermute | solution.py:48
  20.1 1.8 %collective-permute-start.6 = (bf16[1792,128]{1,0:T(8,128)(2,1)S(1)}, bf16[1792,128]{1,0:T(8,128)(2,1)S(1)}, u32[]{:S(2)}, u32[]{:S(2)}) collective-permute-start(bf16[1792,128]{1,0:T(8,128)(2,1)S(1)} %constant_dynamic-slice_fusion), channel_id=1, source_target_pairs={{0,16},{1,65},{2,18},{3,67},{4,20},{5,69},{6,22},{7,71},{8,24},{9,... | collective-permute-start | bytes 1376264 | tf_op jit(solution)/shard_map/ppermute | solution.py:48
  21.9 4.6 %collective-permute-done.4 = bf16[1792,128]{1,0:T(8,128)(2,1)S(1)} collective-permute-done((bf16[1792,128]{1,0:T(8,128)(2,1)S(1)}, bf16[1792,128]{1,0:T(8,128)(2,1)S(1)}, u32[]{:S(2)}, u32[]{:S(2)}) %collective-permute-start.4) | collective-permute-done | bytes 458784 | tf_op jit(solution)/shard_map/ppermute | solution.py:48
  26.7 0.6 gather_fusion
  27.6 0.2 select_reduce_fusion.1
  27.7 3.3 %collective-permute-done.5 = bf16[1792,128]{1,0:T(8,128)(2,1)S(1)} collective-permute-done((bf16[1792,128]{1,0:T(8,128)(2,1)S(1)}, bf16[1792,128]{1,0:T(8,128)(2,1)S(1)}, u32[]{:S(2)}, u32[]{:S(2)}) %collective-permute-start.5) | collective-permute-done | bytes 458784 | tf_op jit(solution)/shard_map/ppermute | solution.py:48
  31.0 1.8 %collective-permute-done.6 = bf16[1792,128]{1,0:T(8,128)(2,1)S(1)} collective-permute-done((bf16[1792,128]{1,0:T(8,128)(2,1)S(1)}, bf16[1792,128]{1,0:T(8,128)(2,1)S(1)}, u32[]{:S(2)}, u32[]{:S(2)}) %collective-permute-start.6) | collective-permute-done | bytes 458784 | tf_op jit(solution)/shard_map/ppermute | solution.py:48
  32.9 3.1 %collective-permute-start.8 = (bf16[3584,128]{1,0:T(8,128)(2,1)S(1)}, bf16[3584,128]{1,0:T(8,128)(2,1)S(1)}, u32[]{:S(2)}, u32[]{:S(2)}) collective-permute-start(bf16[3584,128]{1,0:T(8,128)(2,1)S(1)} %constant_dynamic-update-slice_fusion.7.refs_1_), channel_id=1, source_target_pairs={{0,96},{1,25},{2,98},{3,27},{4,100},{5,29},{6,102},{7,31},{8,104},... | collective-permute-start | bytes 2752520 | tf_op jit(solution)/shard_map/ppermute | solution.py:48
  36.0 0.6 collective-permute-start.10
  36.6 2.7 %collective-permute-start.11 = (bf16[3584,128]{1,0:T(8,128)(2,1)S(1)}, bf16[3584,128]{1,0:T(8,128)(2,1)}, u32[]{:S(2)}, u32[]{:S(2)}) collective-permute-start(bf16[3584,128]{1,0:T(8,128)(2,1)S(1)} %pad_maximum_fusion.refs_0_), channel_id=1, source_target_pairs={{0,96},{1,25},{2,98},{3,27},{4,100},{5,29},{6,102},{7,31},{8,104},... | collective-permute-start | bytes 2752520 | tf_op jit(solution)/shard_map/ppermute | solution.py:48
  39.5 12.3 %shard_map.139 = f32[2,256]{1,0:T(2,128)S(1)} custom-call(s32[2,256]{1,0:T(2,128)S(1)} %get-tuple-element.63.local_ids, bf16[3584,128]{1,0:T(8,128)(2,1)S(1)} %pad_maximum_fusion.refs_0_, bf16[3584,128]{1,0:T(8,128)(2,1)S(1)} %constant_dynamic-update-slice_fusion.7.refs_1_, bf16[2000,3584]{1,0:T(8,128)(2,1)} %bitcast.12, ...), custom_call_target="tpu_custom_call" | custom-call | flops 7340032000 | bytes 28672000 | tf_op jit(solution)/shard_map/pallas_call | solution.py:143
  51.9 3.2 %collective-permute-start.13 = (bf16[3584,128]{1,0:T(8,128)(2,1)S(1)}, bf16[3584,128]{1,0:T(8,128)(2,1)S(1)}, u32[]{:S(2)}, u32[]{:S(2)}) collective-permute-start(bf16[3584,128]{1,0:T(8,128)(2,1)S(1)} %collective-permute-done.8.refs_1_), channel_id=1, source_target_pairs={{0,96},{1,25},{2,98},{3,27},{4,100},{5,29},{6,102},{7,31},{8,104},... | collective-permute-start | bytes 2752520 | tf_op jit(solution)/shard_map/ppermute | solution.py:48
  55.1 12.2 %shard_map.140 = f32[2,256]{1,0:T(2,128)S(1)} custom-call(s32[2,256]{1,0:T(2,128)S(1)} %get-tuple-element.62.local_ids, bf16[3584,128]{1,0:T(8,128)(2,1)} %collective-permute-done.7.refs_0_, bf16[3584,128]{1,0:T(8,128)(2,1)S(1)} %collective-permute-done.8.refs_1_, bf16[2000,3584]{1,0:T(8,128)(2,1)} %bitcast.13, ...), custom_call_target="tpu_custom_call" | custom-call | flops 7340032000 | bytes 28672000 | tf_op jit(solution)/shard_map/pallas_call | solution.py:143
  67.3 3.0 %collective-permute-done.12.refs_2_ = bf16[3584,128]{1,0:T(8,128)(2,1)S(1)} collective-permute-done((bf16[3584,128]{1,0:T(8,128)(2,1)}, bf16[3584,128]{1,0:T(8,128)(2,1)S(1)}, u32[]{:S(2)}, u32[]{:S(2)}) %collective-permute-start.12) | collective-permute-done | bytes 917536 | tf_op jit(solution)/shard_map/ppermute | solution.py:48
  70.3 20.6 %shard_map.141 = f32[2,512]{1,0:T(2,128)S(1)} custom-call(s32[2,512]{1,0:T(2,128)S(1)} %slice.34.local_ids, bf16[3584,128]{1,0:T(8,128)(2,1)} %collective-permute-done.10.refs_0_, bf16[3584,128]{1,0:T(8,128)(2,1)} %collective-permute-done.11.refs_1_, bf16[3584,128]{1,0:T(8,128)(2,1)S(1)} %collective-permute-done.12.refs_2_, ...), custom_call_target="tpu_custom_call" | custom-call | flops 14680064000 | bytes 28672000 | tf_op jit(solution)/shard_map/pallas_call | solution.py:143
  91.0 0.6 gather_fusion.1
  91.8 16.2 %all_to_all.5 = f32[64,2,1024]{2,1,0:T(2,128)S(1)} all-to-all(f32[64,2,1024]{2,1,0:T(2,128)S(1)} %broadcast_in_dim.87), channel_id=1, replica_groups=mesh['tok_0'=4,'tok_1'=4,'voc_0'=4,'voc_1'=2] {'tok_0','tok_1','voc_0'}, dimensions={0} | all-to-all | bytes 1048576 | tf_op jit(solution)/shard_map/all_to_all | solution.py:208
  108.1 0.5 slice_reduce_fusion.1
  108.8 1.1 collective-permute-done.14
  109.9 0.2 select_reduce_fusion
  110.3 1.1 fusion.13
  112.0 0.5 dynamic-slice_bitcast_fusion
  (68 shorter events, 2.0 us)
Async XLA Ops:
  0.6 1.6 %collective-permute-start = (bf16[448,128]{1,0:T(8,128)(2,1)}, bf16[448,128]{1,0:T(8,128)(2,1)S(1)}, u32[]{:S(2)}, u32[]{:S(2)}) collective-permute-start(bf16[448,128]{1,0:T(8,128)(2,1)} %bitcast.15), channel_id=1, source_target_pairs={{0,1},{1,0},{2,3},{3,2},{4,5},{5,4},{6,7},{7,6},{8,9},{9,8},{10,11... | collective-permute-start | bytes 344072 | tf_op jit(solution)/shard_map/ppermute | solution.py:168
  2.2 37.2 %collective-permute-start.9 = (bf16[2000,3584]{1,0:T(8,128)(2,1)}, bf16[2000,3584]{1,0:T(8,128)(2,1)}, u32[]{:S(2)}, u32[]{:S(2)}) collective-permute-start(bf16[2000,3584]{1,0:T(8,128)(2,1)} %bitcast.11), channel_id=1, source_target_pairs={{0,1},{1,0},{2,3},{3,2},{4,5},{5,4},{6,7},{7,6},{8,9},{9,8},{10,11... | collective-permute-start | bytes 43008008 | tf_op jit(solution)/shard_map/ppermute | solution.py:170
  3.7 8.3 %collective-permute-start.1 = (bf16[448,128]{1,0:T(8,128)(2,1)S(1)}, bf16[448,128]{1,0:T(8,128)(2,1)S(1)}, u32[]{:S(2)}, u32[]{:S(2)}) collective-permute-start(bf16[448,128]{1,0:T(8,128)(2,1)S(1)} %get-tuple-element.54), channel_id=1, source_target_pairs={{0,6},{2,0},{4,2},{6,4},{1,7},{3,1},{5,3},{7,5},{8,14},{10,8},{12,... | collective-permute-start | bytes 344072 | tf_op jit(solution)/shard_map/ppermute | solution.py:175
  6.6 7.5 %collective-permute-start.2 = (bf16[448,128]{1,0:T(8,128)(2,1)S(1)}, bf16[448,128]{1,0:T(8,128)(2,1)S(1)}, u32[]{:S(2)}, u32[]{:S(2)}) collective-permute-start(bf16[448,128]{1,0:T(8,128)(2,1)S(1)} %get-tuple-element.54), channel_id=1, source_target_pairs={{0,4},{2,6},{4,0},{6,2},{1,5},{3,7},{5,1},{7,3},{8,12},{10,14},{12... | collective-permute-start | bytes 344072 | tf_op jit(solution)/shard_map/ppermute | solution.py:175
  7.4 8.3 %collective-permute-start.3 = (bf16[448,128]{1,0:T(8,128)(2,1)S(1)}, bf16[448,128]{1,0:T(8,128)(2,1)S(1)}, u32[]{:S(2)}, u32[]{:S(2)}) collective-permute-start(bf16[448,128]{1,0:T(8,128)(2,1)S(1)} %get-tuple-element.54), channel_id=1, source_target_pairs={{0,2},{2,4},{4,6},{6,0},{1,3},{3,5},{5,7},{7,1},{8,10},{10,12},{12... | collective-permute-start | bytes 344072 | tf_op jit(solution)/shard_map/ppermute | solution.py:175
  14.2 12.4 %copy-start = (s32[2048]{0:T(1024)S(1)}, s32[2048]{0:T(1024)}, u32[]{:S(2)}) copy-start(s32[2048]{0:T(1024)} %param.14) | copy-start | bytes 24580
  14.2 12.5 %copy-start.6 = (s32[16]{0:T(128)S(1)}, s32[16]{0:T(128)}, u32[]{:S(2)}) copy-start(s32[16]{0:T(128)} %constant.140.clone) | copy-start | bytes 196
  14.2 12.4 %copy-start.7 = (s32[16]{0:T(128)S(1)}, s32[16]{0:T(128)}, u32[]{:S(2)}) copy-start(s32[16]{0:T(128)} %constant.141.clone) | copy-start | bytes 196
  15.7 11.8 %copy-start.4 = (s32[16]{0:T(128)S(1)}, s32[16]{0:T(128)}, u32[]{:S(2)}) copy-start(s32[16]{0:T(128)} %constant.142.clone) | copy-start | bytes 196
  15.8 11.8 %copy-start.5 = (s32[16]{0:T(128)S(1)}, s32[16]{0:T(128)}, u32[]{:S(2)}) copy-start(s32[16]{0:T(128)} %constant.143.clone) | copy-start | bytes 196
  15.8 11.8 %copy-start.8 = (s32[16]{0:T(128)S(1)}, s32[16]{0:T(128)}, u32[]{:S(2)}) copy-start(s32[16]{0:T(128)} %constant.148) | copy-start | bytes 196
  15.9 10.6 %collective-permute-start.4 = (bf16[1792,128]{1,0:T(8,128)(2,1)S(1)}, bf16[1792,128]{1,0:T(8,128)(2,1)S(1)}, u32[]{:S(2)}, u32[]{:S(2)}) collective-permute-start(bf16[1792,128]{1,0:T(8,128)(2,1)S(1)} %constant_dynamic-slice_fusion), channel_id=1, source_target_pairs={{0,8},{1,33},{2,10},{3,35},{4,12},{5,37},{6,14},{7,39},{8,16},{9,4... | collective-permute-start | bytes 1376264 | tf_op jit(solution)/shard_map/ppermute | solution.py:48
  17.9 13.2 %collective-permute-start.5 = (bf16[1792,128]{1,0:T(8,128)(2,1)S(1)}, bf16[1792,128]{1,0:T(8,128)(2,1)S(1)}, u32[]{:S(2)}, u32[]{:S(2)}) collective-permute-start(bf16[1792,128]{1,0:T(8,128)(2,1)S(1)} %constant_dynamic-slice_fusion), channel_id=1, source_target_pairs={{0,24},{1,97},{2,26},{3,99},{4,28},{5,101},{6,30},{7,103},{8,0},{9... | collective-permute-start | bytes 1376264 | tf_op jit(solution)/shard_map/ppermute | solution.py:48
  20.1 12.7 %collective-permute-start.6 = (bf16[1792,128]{1,0:T(8,128)(2,1)S(1)}, bf16[1792,128]{1,0:T(8,128)(2,1)S(1)}, u32[]{:S(2)}, u32[]{:S(2)}) collective-permute-start(bf16[1792,128]{1,0:T(8,128)(2,1)S(1)} %constant_dynamic-slice_fusion), channel_id=1, source_target_pairs={{0,16},{1,65},{2,18},{3,67},{4,20},{5,69},{6,22},{7,71},{8,24},{9,... | collective-permute-start | bytes 1376264 | tf_op jit(solution)/shard_map/ppermute | solution.py:48
  32.9 18.8 %collective-permute-start.8 = (bf16[3584,128]{1,0:T(8,128)(2,1)S(1)}, bf16[3584,128]{1,0:T(8,128)(2,1)S(1)}, u32[]{:S(2)}, u32[]{:S(2)}) collective-permute-start(bf16[3584,128]{1,0:T(8,128)(2,1)S(1)} %constant_dynamic-update-slice_fusion.7.refs_1_), channel_id=1, source_target_pairs={{0,96},{1,25},{2,98},{3,27},{4,100},{5,29},{6,102},{7,31},{8,104},... | collective-permute-start | bytes 2752520 | tf_op jit(solution)/shard_map/ppermute | solution.py:48
  36.0 15.7 %collective-permute-start.7 = (bf16[3584,128]{1,0:T(8,128)(2,1)S(1)}, bf16[3584,128]{1,0:T(8,128)(2,1)}, u32[]{:S(2)}, u32[]{:S(2)}) collective-permute-start(bf16[3584,128]{1,0:T(8,128)(2,1)S(1)} %pad_maximum_fusion.refs_0_), channel_id=1, source_target_pairs={{0,32},{1,9},{2,34},{3,11},{4,36},{5,13},{6,38},{7,15},{8,40},{9,1... | collective-permute-start | bytes 2752520 | tf_op jit(solution)/shard_map/ppermute | solution.py:48
  36.0 31.3 %collective-permute-start.10 = (bf16[3584,128]{1,0:T(8,128)(2,1)S(1)}, bf16[3584,128]{1,0:T(8,128)(2,1)}, u32[]{:S(2)}, u32[]{:S(2)}) collective-permute-start(bf16[3584,128]{1,0:T(8,128)(2,1)S(1)} %constant_dynamic-update-slice_fusion.7.refs_1_), channel_id=1, source_target_pairs={{0,32},{1,9},{2,34},{3,11},{4,36},{5,13},{6,38},{7,15},{8,40},{9,1... | collective-permute-start | bytes 2752520 | tf_op jit(solution)/shard_map/ppermute | solution.py:48
  36.6 30.7 %collective-permute-start.11 = (bf16[3584,128]{1,0:T(8,128)(2,1)S(1)}, bf16[3584,128]{1,0:T(8,128)(2,1)}, u32[]{:S(2)}, u32[]{:S(2)}) collective-permute-start(bf16[3584,128]{1,0:T(8,128)(2,1)S(1)} %pad_maximum_fusion.refs_0_), channel_id=1, source_target_pairs={{0,96},{1,25},{2,98},{3,27},{4,100},{5,29},{6,102},{7,31},{8,104},... | collective-permute-start | bytes 2752520 | tf_op jit(solution)/shard_map/ppermute | solution.py:48
  51.8 18.5 %collective-permute-start.12 = (bf16[3584,128]{1,0:T(8,128)(2,1)}, bf16[3584,128]{1,0:T(8,128)(2,1)S(1)}, u32[]{:S(2)}, u32[]{:S(2)}) collective-permute-start(bf16[3584,128]{1,0:T(8,128)(2,1)} %collective-permute-done.7.refs_0_), channel_id=1, source_target_pairs={{0,32},{1,9},{2,34},{3,11},{4,36},{5,13},{6,38},{7,15},{8,40},{9,1... | collective-permute-start | bytes 2752520 | tf_op jit(solution)/shard_map/ppermute | solution.py:48
  51.9 18.4 %collective-permute-start.13 = (bf16[3584,128]{1,0:T(8,128)(2,1)S(1)}, bf16[3584,128]{1,0:T(8,128)(2,1)S(1)}, u32[]{:S(2)}, u32[]{:S(2)}) collective-permute-start(bf16[3584,128]{1,0:T(8,128)(2,1)S(1)} %collective-permute-done.8.refs_1_), channel_id=1, source_target_pairs={{0,96},{1,25},{2,98},{3,27},{4,100},{5,29},{6,102},{7,31},{8,104},... | collective-permute-start | bytes 2752520 | tf_op jit(solution)/shard_map/ppermute | solution.py:48
  90.9 17.9 %copy-start.3 = (s32[16]{0:T(128)S(1)}, s32[16]{0:T(128)}, u32[]{:S(2)}) copy-start(s32[16]{0:T(128)} %param.15) | copy-start | bytes 196
  90.9 19.1 %copy-start.1 = (s32[16]{0:T(128)S(1)}, s32[16]{0:T(128)}, u32[]{:S(2)}) copy-start(s32[16]{0:T(128)} %param.16) | copy-start | bytes 196
  90.9 19.2 %copy-start.2 = (f32[16]{0:T(128)S(1)}, f32[16]{0:T(128)}, u32[]{:S(2)}) copy-start(f32[16]{0:T(128)} %param.17) | copy-start | bytes 196
  108.7 1.2 %collective-permute-start.14 = (f32[16,64]{1,0:T(8,128)S(1)}, f32[16,64]{1,0:T(8,128)S(1)}, u32[]{:S(2)}, u32[]{:S(2)}) collective-permute-start(f32[16,64]{1,0:T(8,128)S(1)} %sub.86), channel_id=1, source_target_pairs={{0,1},{1,0},{2,3},{3,2},{4,5},{5,4},{6,7},{7,6},{8,9},{9,8},{10,11... | collective-permute-start | bytes 12296 | tf_op jit(solution)/shard_map/ppermute | solution.py:212
